TPU v7x, 32 devices: a whole 2x2x4 slice. The times are simulated.
32 devices in a mesh: grp: 2 (over y), row: 4 (over z), col: 2 (over x), chan: 2 (over core).
Axes of the slice: x: 2, y: 2, z: 4, core: 2. Of those that a mesh axis runs over, the one named last changes fastest.
Arguments:
- pair: bfloat16 [128, 64, 128], P(('grp', 'row'), 'col'), parts along dimension 0, may hold values from -6 to 6
- window_start: int32 [2], P('grp'), parts along dimension 0, may hold values from 0 to 960
- residue_mask: int32 [2048], P('grp'), parts along dimension 0, may hold values 0 or 1
- in_gain: float32 [2, 128], replicated, may hold values from 0.25 to 1.75
- in_proj: bfloat16 [2, 128, 4, 128], P(None, None, None, 'chan'), may hold values from -0.5 to 0.5
- gate_proj: bfloat16 [2, 128, 128], replicated, may hold values from -0.5 to 0.5
- out_gain: float32 [2, 128], replicated, may hold values from 0.25 to 1.75
- out_proj: bfloat16 [2, 128, 128], replicated, may hold values from -0.5 to 0.5
- cotangent: bfloat16 [128, 64, 128], P(('grp', 'row'), ('col', 'chan')), parts along dimension 0, may hold values from -6 to 6
Outputs:
- new_pair: bfloat16 [128, 64, 128], P(('grp', 'row'), ('col', 'chan')), parts along dimension 0
- pair_grad: float32 [128, 64, 128], P(('grp', 'row'), ('col', 'chan')), parts along dimension 0
There are 2 independent parts, one for each index of `grp`. A program takes and returns all parts, laid end to end along the dimension named above; an argument that names none is the same for every part. Nothing has to cross between parts.
Inputs may be any that keep to these rules, and one draw needn't show every extreme that they name: The window of 64 residues from window_start lies inside the complex.
All inputs are finite; a program needn't handle non-finite values.
Results may differ from a plain program's by a relative error of at most 0.013.
Values may be sent and summed in bfloat16 or wider, within the bound.
A program may use at most 64 MiB of HBM per device.

v0:
```python
import jax
import jax.numpy as jnp
from jax import lax
from jax.sharding import PartitionSpec as P


def layer_norm(values, norm_gain):
    center = values - jnp.mean(values, axis=-1, keepdims=True)
    spread = jnp.mean(center * center, axis=-1, keepdims=True)
    return center * lax.rsqrt(spread + 1e-05) * norm_gain


def gated_half(projected, pair_mask):
    return jax.nn.sigmoid(projected[0]) * projected[1] * pair_mask


def gated_pair(projected, pair_mask):
    return (gated_half(projected[0:2], pair_mask), gated_half(projected[2:4], pair_mask))


def project_pair(tile_values, norm_gain, weight):
    normed = layer_norm(tile_values.astype(jnp.float32), norm_gain).astype(jnp.bfloat16)
    return jnp.einsum("ijc,cgh->ghij", normed, weight, preferred_element_type=jnp.float32)


def finish_update(hidden, current, norm_gain, gate_weight, hidden_gain, out_weight):
    normed = layer_norm(current, norm_gain).astype(jnp.bfloat16)
    gate = jax.nn.sigmoid(
        jnp.einsum("ijc,cd->ijd", normed, gate_weight, preferred_element_type=jnp.float32)
    )
    scaled = layer_norm(hidden, hidden_gain).astype(jnp.bfloat16)
    update = jnp.einsum("ijh,hc->ijc", scaled, out_weight, preferred_element_type=jnp.float32)
    return (current + gate * update, gate, update)


def finish_backward(
    hidden, current, norm_gain, gate_weight, hidden_gain, out_weight, grad, gate, update
):
    d_update = grad * gate
    d_logit = grad * update * gate * (1.0 - gate)
    d_scaled = jnp.einsum(
        "ijc,hc->ijh", d_update, out_weight.astype(jnp.float32), precision=lax.Precision.HIGHEST
    )
    d_normed = jnp.einsum(
        "ijd,cd->ijc", d_logit, gate_weight.astype(jnp.float32), precision=lax.Precision.HIGHEST
    )
    _, back_hidden = jax.vjp(lambda values: layer_norm(values, hidden_gain), hidden)
    _, back_current = jax.vjp(lambda values: layer_norm(values, norm_gain), current)
    (d_hidden,) = back_hidden(d_scaled)
    (d_current,) = back_current(d_normed)
    return (d_hidden.astype(jnp.bfloat16), grad + d_current)


def entry_backward(tile_values, norm_gain, weight, projected, pair_mask, d_left, d_right):
    _, back_gate = jax.vjp(lambda values: gated_pair(values, pair_mask), projected)
    (d_projected,) = back_gate((d_left, d_right))
    d_entry = jnp.einsum(
        "ghij,cgh->ijc", d_projected, weight.astype(jnp.float32), precision=lax.Precision.HIGHEST
    )
    _, back_norm = jax.vjp(
        lambda values: layer_norm(values, norm_gain), tile_values.astype(jnp.float32)
    )
    (d_tile,) = back_norm(d_entry)
    return lax.psum_scatter(
        d_tile.astype(jnp.bfloat16), "chan", scatter_dimension=1, tiled=True
    ).astype(jnp.float32)


def split_cells(hidden):
    return lax.all_to_all(hidden, "chan", split_axis=1, concat_axis=2, tiled=True)


def split_channels(d_hidden):
    return lax.all_to_all(d_hidden, "chan", split_axis=2, concat_axis=1, tiled=True)


def shards(
    pair, window_start, residue_mask, in_gain, in_proj, gate_proj, out_gain, out_proj, cotangent
):
    height = pair.shape[0]
    breadth = pair.shape[1]
    half_width = breadth // lax.axis_size("chan")
    window_len = height * lax.axis_size("row")
    row_anchor = lax.axis_index("row") * height
    col_anchor = lax.axis_index("col") * breadth
    cell_anchor = lax.axis_index("chan") * half_width
    window_mask = lax.dynamic_slice_in_dim(residue_mask, window_start[0], window_len).astype(
        jnp.float32
    )
    row_mask = lax.dynamic_slice_in_dim(window_mask, row_anchor, height)
    col_mask = lax.dynamic_slice_in_dim(window_mask, col_anchor, breadth)
    pair_mask = row_mask[:, None] * col_mask[None, :]
    pair_half = lax.dynamic_slice_in_dim(pair, cell_anchor, half_width, 1).astype(jnp.float32)
    projected_zero = project_pair(pair, in_gain[0], in_proj[0])
    left_f, right_f = gated_pair(projected_zero, pair_mask)
    left_zero = left_f.astype(jnp.bfloat16)
    right_zero = right_f.astype(jnp.bfloat16)
    right_rows = lax.all_gather(right_zero, "row", axis=1, tiled=True)
    picked = right_rows
    summed = lax.psum_scatter(
        jnp.einsum("hik,hjk->jih", left_zero, picked, preferred_element_type=jnp.float32).astype(
            jnp.bfloat16
        ),
        "col",
        scatter_dimension=0,
        tiled=True,
    ).astype(jnp.float32)
    hidden_zero = jnp.transpose(summed, (1, 0, 2)).astype(jnp.bfloat16)
    cells_zero = split_cells(hidden_zero).astype(jnp.float32)
    middle_f, gate_zero, update_zero = finish_update(
        cells_zero, pair_half, in_gain[0], gate_proj[0], out_gain[0], out_proj[0]
    )
    middle_half = middle_f.astype(jnp.bfloat16)
    middle = lax.all_gather(middle_half, "chan", axis=1, tiled=True)
    projected_one = project_pair(middle, in_gain[1], in_proj[1])
    left_f, right_f = gated_pair(projected_one, pair_mask)
    left_one = left_f.astype(jnp.bfloat16)
    right_one = right_f.astype(jnp.bfloat16)
    left_cols = lax.all_gather(left_one, "col", axis=2, tiled=True)
    picked = left_cols
    hidden_one = lax.psum_scatter(
        jnp.einsum("hki,hkj->ijh", picked, right_one, preferred_element_type=jnp.float32).astype(
            jnp.bfloat16
        ),
        "row",
        scatter_dimension=0,
        tiled=True,
    )
    cells_one = split_cells(hidden_one).astype(jnp.float32)
    middle_part = middle_half.astype(jnp.float32)
    final_f, gate_one, update_one = finish_update(
        cells_one, middle_part, in_gain[1], gate_proj[1], out_gain[1], out_proj[1]
    )
    new_pair = final_f.astype(jnp.bfloat16)
    pair_rows = lax.all_gather(pair, "row", axis=0, tiled=True)
    rows_mask = window_mask[:, None] * col_mask[None, :]
    right_rows = gated_half(
        project_pair(pair_rows, in_gain[0], in_proj[0][:, 2:4]), rows_mask
    ).astype(jnp.bfloat16)
    middle_cols = lax.all_gather(middle, "col", axis=1, tiled=True)
    cols_mask = row_mask[:, None] * window_mask[None, :]
    left_cols = gated_half(
        project_pair(middle_cols, in_gain[1], in_proj[1][:, 0:2]), cols_mask
    ).astype(jnp.bfloat16)
    grad_two = cotangent.astype(jnp.float32)
    d_cells_one, direct_one = finish_backward(
        cells_one,
        middle_part,
        in_gain[1],
        gate_proj[1],
        out_gain[1],
        out_proj[1],
        grad_two,
        gate_one,
        update_one,
    )
    d_hidden_one = split_channels(d_cells_one)
    d_hidden_rows = lax.all_gather(d_hidden_one, "row", axis=0, tiled=True)
    d_right_one = jnp.einsum(
        "hki,ijh->hkj", left_cols, d_hidden_rows, preferred_element_type=jnp.float32
    )
    picked = d_hidden_rows
    d_left_one = jnp.transpose(
        lax.psum_scatter(
            jnp.einsum(
                "hkj,ijh->ihk", right_one, picked, preferred_element_type=jnp.float32
            ).astype(jnp.bfloat16),
            "col",
            scatter_dimension=0,
            tiled=True,
        ).astype(jnp.float32),
        (1, 2, 0),
    )
    grad_one = direct_one + entry_backward(
        middle, in_gain[1], in_proj[1], projected_one, pair_mask, d_left_one, d_right_one
    )
    d_cells_zero, direct_zero = finish_backward(
        cells_zero,
        pair_half,
        in_gain[0],
        gate_proj[0],
        out_gain[0],
        out_proj[0],
        grad_one,
        gate_zero,
        update_zero,
    )
    d_hidden_zero = split_channels(d_cells_zero)
    d_hidden_cols = lax.all_gather(d_hidden_zero, "col", axis=1, tiled=True)
    d_left_zero = jnp.einsum(
        "ijh,hjk->hik", d_hidden_cols, right_rows, preferred_element_type=jnp.float32
    )
    picked = d_hidden_cols
    d_right_zero = jnp.transpose(
        lax.psum_scatter(
            jnp.einsum(
                "ijh,hik->jhk", picked, left_zero, preferred_element_type=jnp.float32
            ).astype(jnp.bfloat16),
            "row",
            scatter_dimension=0,
            tiled=True,
        ).astype(jnp.float32),
        (1, 0, 2),
    )
    pair_grad = direct_zero + entry_backward(
        pair, in_gain[0], in_proj[0], projected_zero, pair_mask, d_left_zero, d_right_zero
    )
    return (new_pair, pair_grad)


def solution(mesh):
    placed = (
        P(("grp", "row"), "col", None),
        P("grp"),
        P("grp"),
        P(),
        P(None, None, None, "chan"),
        P(),
        P(),
        P(),
        P(("grp", "row"), ("col", "chan"), None),
    )
    return jax.shard_map(
        shards,
        mesh=mesh,
        in_specs=placed,
        out_specs=(
            P(("grp", "row"), ("col", "chan"), None),
            P(("grp", "row"), ("col", "chan"), None),
        ),
        check_vma=False,
    )
```

profile of v0, /device:TPU:3, one launch (start us, length us, event | category | flops | bytes accessed | tf_op | source)
XLA Modules:
  0.0 245.1 jit_solution(17829603109160530309)
XLA Ops:
  7.2 1.2 slice_bitcast_fusion.12
  8.5 1.0 convert_reduce_fusion.3
  9.5 1.2 fusion.51
  11.4 0.8 dynamic-slice_convert_fusion
  12.4 1.3 convolution_bitcast_fusion.3
  13.8 14.5 %all_gather.21 = bf16[64,64,32]{0,2,1:T(8,128)(2,1)S(1)} all-gather(bf16[64,16,32]{0,2,1:T(8,128)(2,1)S(1)} %get-tuple-element.21), channel_id=1, replica_groups=mesh['grp'=2,'row'=4,'col'=2,'chan'=2] {'row'}, dimensions={1}, use_global_device_ids=true | all-gather | bytes 327680 | tf_op jit(solution)/shard_map/all_gather | solution.py:98
  28.3 1.6 copy.203
  30.8 1.1 copy.205
  33.3 11.9 %all_gather.27 = bf16[64,32,128]{2,1,0:T(8,128)(2,1)S(1)} all-gather(bf16[16,32,128]{2,1,0:T(8,128)(2,1)S(1)} %copy-done), channel_id=1, replica_groups=mesh['grp'=2,'row'=4,'col'=2,'chan'=2] {'row'}, dimensions={0}, use_global_device_ids=true | all-gather | bytes 655360 | tf_op jit(solution)/shard_map/all_gather | solution.py:135
  49.1 1.8 copy.235
  50.9 0.9 bitcast_bitcast_fusion
  52.0 9.9 %all_to_all.54 = bf16[2,2,8192]{2,1,0:T(2,128)(2,1)S(1)} all-to-all(bf16[2,2,8192]{2,1,0:T(2,128)(2,1)S(1)} %reshape.341), channel_id=1, replica_groups=mesh['grp'=2,'row'=4,'col'=2,'chan'=2] {'chan'}, dimensions={0} | all-to-all | bytes 131072 | tf_op jit(solution)/shard_map/all_to_all | solution.py:70
  64.3 0.9 convert_reduce_fusion.4
  65.2 1.9 all_gather.22
  67.2 5.4 %all_gather.24 = bf16[16,64,128]{2,1,0:T(8,128)(2,1)S(1)} all-gather(bf16[16,32,128]{2,1,0:T(8,128)(2,1)S(1)} %all_gather.22), channel_id=1, replica_groups=mesh['grp'=2,'row'=4,'col'=2,'chan'=2] {'col'}, dimensions={1}, use_global_device_ids=true | all-gather | bytes 393216 | tf_op jit(solution)/shard_map/all_gather | solution.py:140
  73.3 1.2 convolution_bitcast_fusion.1
  74.5 0.9 fusion.36
  75.4 0.9 copy.222
  77.5 4.6 %all_gather.23 = bf16[64,16,64]{0,2,1:T(8,128)(2,1)} all-gather(bf16[64,16,32]{0,2,1:T(8,128)(2,1)S(1)} %get-tuple-element.18), channel_id=1, replica_groups=mesh['grp'=2,'row'=4,'col'=2,'chan'=2] {'col'}, dimensions={2}, use_global_device_ids=true | all-gather | bytes 196608 | tf_op jit(solution)/shard_map/all_gather | solution.py:119
  82.1 1.9 copy.210
  84.0 2.1 fusion.2
  86.1 2.9 %copy.211 = bf16[64,32,64]{2,1,0:T(8,128)(2,1)} copy(bf16[64,32,64]{0,1,2:T(8,128)(2,1)} %fusion.2) | data formatting | bytes 524288 | tf_op jit(solution)/shard_map/convert_element_type | solution.py:122
  89.3 0.9 copy.226
  90.1 1.1 reshape.309
  92.1 19.1 %reduce-scatter.9.cloned.1.call-done = bf16[16,32,64]{2,1,0:T(8,128)(2,1)} async-done(((bf16[64,32,64]{2,1,0:T(8,128)(2,1)}), bf16[16,32,64]{2,1,0:T(8,128)(2,1)}) %reduce-scatter.9.cloned.1.call-update) | async-done | bytes 65552 | tf_op jit(solution)/shard_map/reduce_scatter | solution.py:121
  111.2 1.0 copy.263
  112.3 5.8 %all_to_all.55 = bf16[2,2,8192]{2,1,0:T(2,128)(2,1)S(1)} all-to-all(bf16[2,2,8192]{2,1,0:T(2,128)(2,1)S(1)} %reshape.343), channel_id=1, replica_groups=mesh['grp'=2,'row'=4,'col'=2,'chan'=2] {'chan'}, dimensions={0} | all-to-all | bytes 131072 | tf_op jit(solution)/shard_map/all_to_all | solution.py:70
  118.3 0.9 copy.262
  119.2 1.2 fusion.187
  120.4 1.1 reshape.308
  122.2 0.8 multiply_reduce_fusion
  123.0 1.2 multiply_reduce_fusion.3
  124.8 0.8 add_convert_fusion.3
  125.6 2.0 copy.218
  127.7 1.6 reshape.345
  129.3 3.8 %all_to_all.56 = bf16[2,2,8192]{2,1,0:T(2,128)(2,1)S(1)} all-to-all(bf16[2,2,8192]{2,1,0:T(2,128)(2,1)S(1)} %reshape.345), channel_id=1, replica_groups=mesh['grp'=2,'row'=4,'col'=2,'chan'=2] {'chan'}, dimensions={0} | all-to-all | bytes 131072 | tf_op jit(solution)/shard_map/all_to_all | solution.py:74
  133.1 1.2 reshape.346
  134.2 1.5 copy.243
  136.4 1.1 copy.221
  137.6 20.5 %all_gather.25 = bf16[64,32,64]{1,0,2:T(8,128)(2,1)S(1)} all-gather(bf16[16,32,64]{1,0,2:T(8,128)(2,1)S(1)} %copy.221), channel_id=1, replica_groups=mesh['grp'=2,'row'=4,'col'=2,'chan'=2] {'row'}, dimensions={0}, use_global_device_ids=true | all-gather | bytes 327680 | tf_op jit(solution)/shard_map/all_gather | solution.py:158
  158.1 1.4 fusion.190
  159.5 1.3 fusion.189
  160.8 1.9 copy.225
  162.8 2.0 multiply_convert_fusion
  164.8 1.0 convert_element_type.203
  165.9 0.9 fusion.156
  166.8 1.9 fusion.111
  168.7 1.0 copy.223
  169.7 1.3 multiply_multiply_fusion.5
  171.0 2.1 reduce-scatter.11.cloned.1.call-done
  173.0 1.3 multiply_bitcast_fusion.1
  175.6 1.0 add_convert_fusion.1
  176.7 1.2 fusion.153
  177.9 8.1 %reduce-scatter.13.cloned.1.call-done = bf16[16,16,128]{2,1,0:T(8,128)(2,1)} async-done(((bf16[16,32,128]{2,1,0:T(8,128)(2,1)}), bf16[16,16,128]{2,1,0:T(8,128)(2,1)}) %reduce-scatter.13.cloned.1.call-update) | async-done | bytes 65552 | tf_op jit(solution)/shard_map/reduce_scatter | solution.py:64
  186.0 1.7 fusion.116
  187.7 1.2 multiply_reduce_fusion.2
  190.4 3.6 %all_to_all.57 = bf16[2,2,8192]{2,1,0:T(2,128)(2,1)S(1)} all-to-all(bf16[2,2,8192]{2,1,0:T(2,128)(2,1)S(1)} %reshape.347), channel_id=1, replica_groups=mesh['grp'=2,'row'=4,'col'=2,'chan'=2] {'chan'}, dimensions={0} | all-to-all | bytes 131072 | tf_op jit(solution)/shard_map/all_to_all | solution.py:74
  195.0 5.6 %all_gather.26 = bf16[16,64,64]{2,0,1:T(8,128)(2,1)S(1)} all-gather(bf16[16,32,64]{2,0,1:T(8,128)(2,1)S(1)} %bitcast.330), channel_id=1, replica_groups=mesh['grp'=2,'row'=4,'col'=2,'chan'=2] {'col'}, dimensions={1}, use_global_device_ids=true | all-gather | bytes 196608 | tf_op jit(solution)/shard_map/all_gather | solution.py:189
  201.4 1.8 copy.233
  204.5 20.3 %reduce-scatter.15.cloned.1.call-done = bf16[16,64,32]{1,2,0:T(8,128)(2,1)} async-done(((bf16[64,64,32]{1,2,0:T(8,128)(2,1)}), bf16[16,64,32]{1,2,0:T(8,128)(2,1)}) %reduce-scatter.15.cloned.1.call-update) | async-done | bytes 65552 | tf_op jit(solution)/shard_map/reduce_scatter | solution.py:195
  224.8 1.2 fusion.87
  227.2 1.0 add_convert_fusion
  228.5 8.1 %reduce-scatter.17.cloned.1.call-done = bf16[16,16,128]{2,1,0:T(8,128)(2,1)} async-done(((bf16[16,32,128]{2,1,0:T(8,128)(2,1)}), bf16[16,16,128]{2,1,0:T(8,128)(2,1)}) %reduce-scatter.17.cloned.1.call-update) | async-done | bytes 65552 | tf_op jit(solution)/shard_map/reduce_scatter | solution.py:64
  236.5 1.7 convert_add_fusion.3
  (204 shorter events, 21.0 us)
Async XLA Ops:
  7.2 43.8 %reduce-scatter.7.cloned.1.call-start = ((), (), s32[]{:S(2)}) async-start(), calls=%async_computation.10 | async-start | bytes 393216 | tf_op jit(solution)/shard_map/reduce_scatter | solution.py:100
  8.5 38.5 %copy-start.48 = (f32[128]{0:T(128)}, f32[128]{0:T(128)S(1)}, u32[]{:S(2)}) copy-start(f32[128]{0:T(128)S(1)} %get-tuple-element.35) | copy-start | bytes 1540
  10.7 3.1 %copy-start.34 = (f32[16,32]{1,0:T(8,128)}, f32[16,32]{1,0:T(8,128)S(1)}, u32[]{:S(2)}) copy-start(f32[16,32]{1,0:T(8,128)S(1)} %fusion.51) | copy-start | bytes 6148
  10.7 3.1 %copy-start.24 = (f32[16,32]{1,0:T(8,128)}, f32[16,32]{1,0:T(8,128)S(1)}, u32[]{:S(2)}) copy-start(f32[16,32]{1,0:T(8,128)S(1)} %fusion.177) | copy-start | bytes 6148
  28.3 3.7 %copy-start.4 = (bf16[2,128,4,64]{1,3,2,0:T(8,128)(2,1)S(1)}, bf16[2,128,4,64]{1,3,2,0:T(8,128)(2,1)}, u32[]{:S(2)}) copy-start(bf16[2,128,4,64]{1,3,2,0:T(8,128)(2,1)} %param.13) | copy-start | bytes 393220
  28.3 5.0 %copy-start = (bf16[16,32,128]{2,1,0:T(8,128)(2,1)S(1)}, bf16[16,32,128]{2,1,0:T(8,128)(2,1)}, u32[]{:S(2)}) copy-start(bf16[16,32,128]{2,1,0:T(8,128)(2,1)} %param.9) | copy-start | bytes 393220
  29.9 15.4 %copy-start.51 = (f32[2,128]{1,0:T(2,128)S(1)}, f32[2,128]{1,0:T(2,128)}, u32[]{:S(2)}) copy-start(f32[2,128]{1,0:T(2,128)} %param.15) | copy-start | bytes 3076
  31.9 79.3 %reduce-scatter.9.cloned.1.call-start = ((), (), s32[]{:S(2)}) async-start(), calls=%async_computation.11 | async-start | bytes 655360 | tf_op jit(solution)/shard_map/reduce_scatter | solution.py:121
  46.0 18.2 %copy-start.21 = (f32[16,16]{1,0:T(8,128)}, f32[16,16]{1,0:T(8,128)S(1)}, u32[]{:S(2)}) copy-start(f32[16,16]{1,0:T(8,128)S(1)} %broadcast_multiply_fusion.10) | copy-start | bytes 3076
  48.1 16.0 %copy-start.20 = (bf16[2,128,128]{2,1,0:T(8,128)(2,1)S(1)}, bf16[2,128,128]{2,1,0:T(8,128)(2,1)}, u32[]{:S(2)}) copy-start(bf16[2,128,128]{2,1,0:T(8,128)(2,1)} %param.16) | copy-start | bytes 196612
  48.1 16.1 %copy-start.43 = (bf16[2,128,128]{2,1,0:T(8,128)(2,1)S(1)}, bf16[2,128,128]{2,1,0:T(8,128)(2,1)}, u32[]{:S(2)}) copy-start(bf16[2,128,128]{2,1,0:T(8,128)(2,1)} %param.14) | copy-start | bytes 196612
  48.1 16.1 %copy-start.49 = (f32[128]{0:T(128)S(1)}, f32[128]{0:T(128)}, u32[]{:S(2)}) copy-start(f32[128]{0:T(128)} %copy-done.48) | copy-start | bytes 1540
  48.3 2.6 %copy-start.36 = (f32[16,16]{1,0:T(8,128)}, f32[16,16]{1,0:T(8,128)S(1)}, u32[]{:S(2)}) copy-start(f32[16,16]{1,0:T(8,128)S(1)} %fusion.103) | copy-start | bytes 3076
  50.9 21.7 %copy-start.31 = (f32[16,16]{1,0:T(8,128)}, f32[16,16]{1,0:T(8,128)S(1)}, u32[]{:S(2)}) copy-start(f32[16,16]{1,0:T(8,128)S(1)} %fusion.176) | copy-start | bytes 3076
  62.3 0.6 copy-start.18
  62.5 0.6 copy-start.38
  63.1 0.6 copy-start.28
  64.2 11.2 %copy-start.12 = (f32[16,16,128]{2,1,0:T(8,128)}, f32[16,16,128]{2,1,0:T(8,128)S(1)}, u32[]{:S(2)}) copy-start(f32[16,16,128]{2,1,0:T(8,128)S(1)} %fusion.161) | copy-start | bytes 393220
  65.2 26.6 %copy-start.2 = (bf16[16,16,128]{2,1,0:T(8,128)(2,1)}, bf16[16,16,128]{2,1,0:T(8,128)(2,1)S(1)}, u32[]{:S(2)}) copy-start(bf16[16,16,128]{2,1,0:T(8,128)(2,1)S(1)} %get-tuple-element.5) | copy-start | bytes 196612
  67.2 9.4 %copy-start.46 = (f32[128]{0:T(128)S(1)}, f32[128]{0:T(128)}, u32[]{:S(2)}) copy-start(f32[128]{0:T(128)} %get-tuple-element.34) | copy-start | bytes 1540
  72.6 4.4 %copy-start.15 = (f32[16,32]{1,0:T(8,128)}, f32[16,32]{1,0:T(8,128)S(1)}, u32[]{:S(2)}) copy-start(f32[16,32]{1,0:T(8,128)S(1)} %broadcast_multiply_fusion.5) | copy-start | bytes 6148
  76.6 9.5 %copy-start.40 = (f32[16,32]{1,0:T(8,128)}, f32[16,32]{1,0:T(8,128)S(1)}, u32[]{:S(2)}) copy-start(f32[16,32]{1,0:T(8,128)S(1)} %fusion.55) | copy-start | bytes 6148
  76.7 9.5 %copy-start.26 = (f32[16,32]{1,0:T(8,128)}, f32[16,32]{1,0:T(8,128)S(1)}, u32[]{:S(2)}) copy-start(f32[16,32]{1,0:T(8,128)S(1)} %fusion.180) | copy-start | bytes 6148
  82.1 9.4 %copy-start.44 = (bf16[2,128,128]{2,1,0:T(8,128)(2,1)S(1)}, bf16[2,128,128]{2,1,0:T(8,128)(2,1)}, u32[]{:S(2)}) copy-start(bf16[2,128,128]{2,1,0:T(8,128)(2,1)} %param.14) | copy-start | bytes 196612
  89.0 84.0 %reduce-scatter.11.cloned.1.call-start = ((), (), s32[]{:S(2)}) async-start(), calls=%async_computation.12 | async-start | bytes 393216 | tf_op jit(solution)/shard_map/reduce_scatter | solution.py:164
  89.3 2.5 %copy-start.23 = (f32[16,16]{1,0:T(8,128)}, f32[16,16]{1,0:T(8,128)S(1)}, u32[]{:S(2)}) copy-start(f32[16,16]{1,0:T(8,128)S(1)} %broadcast_multiply_fusion.8) | copy-start | bytes 3076
  91.5 20.7 %copy-start.42 = (f32[16,16]{1,0:T(8,128)}, f32[16,16]{1,0:T(8,128)S(1)}, u32[]{:S(2)}) copy-start(f32[16,16]{1,0:T(8,128)S(1)} %fusion.108) | copy-start | bytes 3076
  91.5 0.6 copy-start.33
  92.1 35.6 %copy-start.7 = (f32[16,16,128]{2,1,0:T(8,128)}, f32[16,16,128]{2,1,0:T(8,128)S(1)}, u32[]{:S(2)}) copy-start(f32[16,16,128]{2,1,0:T(8,128)S(1)} %fusion.11) | copy-start | bytes 393220
  122.2 2.3 copy-start.17
  124.2 0.6 copy-start.30
  162.8 23.3 %reduce-scatter.13.cloned.1.call-start = ((), (), s32[]{:S(2)}) async-start(), calls=%async_computation.13 | async-start | bytes 196608 | tf_op jit(solution)/shard_map/reduce_scatter | solution.py:64
  166.8 2.9 %copy-start.9 = (f32[16,16,128]{2,1,0:T(8,128)}, f32[16,16,128]{2,1,0:T(8,128)S(1)}, u32[]{:S(2)}) copy-start(f32[16,16,128]{2,1,0:T(8,128)S(1)} %fusion.156) | copy-start | bytes 393220
  171.0 3.5 %copy-start.5 = (bf16[2,128,4,64]{1,3,2,0:T(8,128)(2,1)S(1)}, bf16[2,128,4,64]{1,3,2,0:T(8,128)(2,1)}, u32[]{:S(2)}) copy-start(bf16[2,128,4,64]{1,3,2,0:T(8,128)(2,1)} %param.13) | copy-start | bytes 393220
  173.0 1.4 copy-start.16
  173.0 1.5 copy-start.47
  174.3 0.9 copy-start.41
  174.3 0.9 copy-start.27
  174.3 2.4 copy-start.3
  174.3 11.7 %copy-start.8 = (f32[16,16,128]{2,1,0:T(8,128)S(1)}, f32[16,16,128]{2,1,0:T(8,128)}, u32[]{:S(2)}) copy-start(f32[16,16,128]{2,1,0:T(8,128)} %copy-done.7) | copy-start | bytes 393220
  174.3 11.7 %copy-start.10 = (f32[16,16,128]{2,1,0:T(8,128)S(1)}, f32[16,16,128]{2,1,0:T(8,128)}, u32[]{:S(2)}) copy-start(f32[16,16,128]{2,1,0:T(8,128)} %copy-done.9) | copy-start | bytes 393220
  174.3 11.7 %copy-start.11 = (bf16[16,16,128]{2,1,0:T(8,128)(2,1)S(1)}, bf16[16,16,128]{2,1,0:T(8,128)(2,1)}, u32[]{:S(2)}) copy-start(bf16[16,16,128]{2,1,0:T(8,128)(2,1)} %param.17) | copy-start | bytes 196612
  175.2 13.8 %copy-start.39 = (f32[16,16]{1,0:T(8,128)S(1)}, f32[16,16]{1,0:T(8,128)}, u32[]{:S(2)}) copy-start(f32[16,16]{1,0:T(8,128)} %copy-done.38) | copy-start | bytes 3076
  175.2 13.8 %copy-start.19 = (f32[16,16]{1,0:T(8,128)S(1)}, f32[16,16]{1,0:T(8,128)}, u32[]{:S(2)}) copy-start(f32[16,16]{1,0:T(8,128)} %copy-done.18) | copy-start | bytes 3076
  175.2 13.8 %copy-start.29 = (f32[16,16]{1,0:T(8,128)S(1)}, f32[16,16]{1,0:T(8,128)}, u32[]{:S(2)}) copy-start(f32[16,16]{1,0:T(8,128)} %copy-done.28) | copy-start | bytes 3076
  176.6 48.1 %reduce-scatter.15.cloned.1.call-start = ((), (), s32[]{:S(2)}) async-start(), calls=%async_computation.14 | async-start | bytes 655360 | tf_op jit(solution)/shard_map/reduce_scatter | solution.py:195
  194.4 8.9 %copy-start.1 = (bf16[64,64,32]{1,2,0:T(8,128)(2,1)S(1)}, bf16[64,64,32]{1,2,0:T(8,128)(2,1)}, u32[]{:S(2)}) copy-start(bf16[64,64,32]{1,2,0:T(8,128)(2,1)} %copy.235) | copy-start | bytes 786436
  201.4 2.6 %copy-start.13 = (f32[16,16,128]{2,1,0:T(8,128)S(1)}, f32[16,16,128]{2,1,0:T(8,128)}, u32[]{:S(2)}) copy-start(f32[16,16,128]{2,1,0:T(8,128)} %copy-done.12) | copy-start | bytes 393220
  203.2 0.9 copy-start.14
  203.2 0.9 copy-start.22
  203.2 0.9 copy-start.45
  203.2 0.9 copy-start.50
  203.2 1.2 copy-start.37
  203.3 33.3 %reduce-scatter.17.cloned.1.call-start = ((), (), s32[]{:S(2)}) async-start(), calls=%async_computation.15 | async-start | bytes 196608 | tf_op jit(solution)/shard_map/reduce_scatter | solution.py:64
  204.5 21.6 %copy-start.6 = (bf16[2,128,4,64]{1,3,2,0:T(8,128)(2,1)S(1)}, bf16[2,128,4,64]{1,3,2,0:T(8,128)(2,1)}, u32[]{:S(2)}) copy-start(bf16[2,128,4,64]{1,3,2,0:T(8,128)(2,1)} %param.13) | copy-start | bytes 393220
  225.9 0.8 copy-start.35
  225.9 0.9 copy-start.25
  226.0 2.2 copy-start.32
Sparse Core Ops, SparseCore 0:
  32.0 13.8 reduce-scatter.6
  89.2 21.9 reduce-scatter.8
  162.9 10.0 reduce-scatter.10
  176.8 9.2 reduce-scatter.12
  203.4 21.3 reduce-scatter.14
  228.3 8.1 reduce-scatter.16
where the time goes:
time: 247 us; the launch traced here: 245 us
  blocking collectives  87.5 us (35%)
  waiting for transfers between devices  57.7 us (23%)
  local copies, waits for them, and re-layouts  39.4 us (16%)
  other arithmetic  26.1 us (11%)
  matrix products  18 us (7%)
  between operations  15.9 us (6%)
    all_gather x1, blocking collectives, shards(): d_hidden_rows = lax.all_gather(d_hidden_one, 'row', axis=0, tiled=True)  20.5 us
    reduce_scatter x1, waiting for transfers between devices, shards(): lax.psum_scatter(jnp.einsum('ijh,hik->jhk', picked, left_zero, preferred_...  20.3 us
    reduce_scatter x1, waiting for transfers between devices, shards(): lax.psum_scatter(jnp.einsum('hki,hkj->ijh', picked, right_one, preferred_...  19.1 us
    reduce_scatter x2, waiting for transfers between devices, entry_backward(): lax.psum_scatter(d_tile.astype(jnp.bfloat16), 'chan', scatter_dimension=1...  16.2 us
    all_to_all x2, blocking collectives, split_cells(): lax.all_to_all(hidden, 'chan', split_axis=1, concat_axis=2, tiled=True)  15.7 us
    all_gather x1, blocking collectives, shards(): right_rows = lax.all_gather(right_zero, 'row', axis=1, tiled=True)  14.5 us
    all_gather x1, blocking collectives, shards(): pair_rows = lax.all_gather(pair, 'row', axis=0, tiled=True)  11.9 us
    all_to_all x2, blocking collectives, split_channels(): lax.all_to_all(d_hidden, 'chan', split_axis=2, concat_axis=1, tiled=True)  7.42 us
  transfers between devices with their start and end apart: 6, of which 5 were waited for; matrix products, arithmetic and copies ran while one was open for 8% of the time, Pallas kernels for 0%

commit v1 on v0

v1 whole, which is shorter than its diff:
```python
import functools

import jax
import jax.numpy as jnp
from jax import lax
from jax.experimental import pallas as pl
from jax.experimental.pallas import tpu as pltpu
from jax.sharding import PartitionSpec as P

F32 = jnp.float32
BF16 = jnp.bfloat16
MESH = pl.DeviceIdType.MESH

A0_ROW, B0_TOQ, A0_COL, B0_COL, B1_COL, A1_TOR, A1_ROW, B1_ROW = range(8)
D1_COL, D1_TOQ, D0_ROW, D0_TOR = range(8, 12)
KINDS = 12


def dot(a, b):
    return lax.dot_general(a, b, (((1,), (0,)), ((), ())), preferred_element_type=F32)


def dot_t(a, b):
    return lax.dot_general(a, b, (((1,), (1,)), ((), ())), preferred_element_type=F32)


def unit(x):
    center = x - jnp.mean(x, axis=-1, keepdims=True)
    inv = lax.rsqrt(jnp.mean(center * center, axis=-1, keepdims=True) + 1e-05)
    return center * inv, inv


def unit_back(hat, inv, d_hat):
    mean = jnp.mean(d_hat, axis=-1, keepdims=True)
    slope = jnp.mean(d_hat * hat, axis=-1, keepdims=True)
    return inv * (d_hat - mean - hat * slope)


def kernel(
    n,
    n_chan,
    pair_ref,
    start_ref,
    residue_ref,
    in_gain_ref,
    in_proj_ref,
    gate_proj_ref,
    out_gain_ref,
    out_proj_ref,
    cot_ref,
    new_ref,
    grad_ref,
    buf,
    stage,
    weight,
    mask_ref,
    lhs_ref,
    acc_ref,
    proj_ref,
    wide_ref,
    send_sem,
    recv_sem,
    weight_send,
    weight_recv,
):
    t = pair_ref.shape[0]
    ch = pair_ref.shape[2]
    hid = weight.shape[2]
    cells = t * t
    r = lax.axis_index("row")
    chan = lax.axis_index("chan")
    q = lax.axis_index("col") * n_chan + chan
    same = r == q

    def at(row, place):
        return {"row": row, "col": place // n_chan, "chan": lax.rem(place, n_chan)}

    def targets(way):
        if way == "row":
            return [(at(r, lax.rem(q + d, n)), False) for d in range(1, n)]
        if way == "col":
            return [(at(lax.rem(r + d, n), q), False) for d in range(1, n)]
        if way == "to_q":
            return [(at(lax.rem(r + d, n), r), d == 0) for d in range(n)]
        return [(at(q, lax.rem(q + d, n)), d == 0) for d in range(n)]

    ways = {
        A0_ROW: "row",
        A1_ROW: "row",
        B1_ROW: "row",
        D0_ROW: "row",
        A0_COL: "col",
        B0_COL: "col",
        B1_COL: "col",
        D1_COL: "col",
        B0_TOQ: "to_q",
        D1_TOQ: "to_q",
        A1_TOR: "to_r",
        D0_TOR: "to_r",
    }

    barrier = pltpu.get_barrier_semaphore()
    for way in ("row", "col", "to_q", "to_r"):
        for device, maybe_self in targets(way):

            def greet(device=device):
                pl.semaphore_signal(barrier, inc=1, device_id=device, device_id_type=MESH)

            if maybe_self:
                pl.when(jnp.logical_not(same))(greet)
            else:
                greet()
    count = 4 * n - 2

    @pl.when(same)
    def _():
        pl.semaphore_wait(barrier, count - 2)

    @pl.when(jnp.logical_not(same))
    def _():
        pl.semaphore_wait(barrier, count)

    def slot_of(kind):
        return q if ways[kind] in ("row", "to_q") else r

    pending = []

    def push(kind, source):
        slot = slot_of(kind)
        for step, (device, maybe_self) in enumerate(targets(ways[kind])):
            copy = pltpu.make_async_remote_copy(
                src_ref=source,
                dst_ref=buf.at[kind, slot],
                send_sem=send_sem.at[kind, step],
                recv_sem=recv_sem.at[kind, slot],
                device_id=device,
                device_id_type=MESH,
            )
            pending.append((copy, maybe_self))
            if maybe_self:
                pl.when(jnp.logical_not(same))(copy.start)
            else:
                copy.start()

    def arrive(kind, slot):
        copy = pltpu.make_async_remote_copy(
            src_ref=buf.at[kind, slot],
            dst_ref=buf.at[kind, slot],
            send_sem=send_sem.at[kind, 0],
            recv_sem=recv_sem.at[kind, slot],
            device_id={"row": r},
            device_id_type=MESH,
        )
        way = ways[kind]
        if way in ("row", "col"):
            pl.when(slot != (q if way == "row" else r))(copy.wait_recv)
        else:
            pl.when(jnp.logical_not(jnp.logical_and(same, slot == r)))(copy.wait_recv)

    part = in_proj_ref.shape[2]
    mine = pl.ds(pl.multiple_of(chan * part, part), part)
    weight_copies = []
    for u in range(2):
        for d in range(1, n_chan):
            copy = pltpu.make_async_remote_copy(
                src_ref=in_proj_ref.at[u],
                dst_ref=weight.at[u, :, mine, :],
                send_sem=weight_send.at[u, d - 1],
                recv_sem=weight_recv.at[u, chan],
                device_id={"chan": lax.rem(chan + d, n_chan)},
                device_id_type=MESH,
            )
            copy.start()
            weight_copies.append(copy)
    weight[:, :, mine, :] = in_proj_ref[...]

    first = start_ref[0]
    rows = lax.broadcasted_iota(jnp.int32, (t, ch), 0)
    col_mask = jnp.zeros((t, ch), F32)
    for j in range(t):
        value = residue_ref[first + q * t + j].astype(F32)
        col_mask = jnp.where(rows == j, value, col_mask)
    for i in range(t):
        mask_ref[i] = col_mask * residue_ref[first + r * t + i].astype(F32)

    def wait_weight(u):
        for d in range(1, n_chan):
            other = lax.rem(chan + d, n_chan)
            theirs = pl.ds(pl.multiple_of(other * part, part), part)
            pltpu.make_async_remote_copy(
                src_ref=in_proj_ref.at[u],
                dst_ref=weight.at[u, :, theirs, :],
                send_sem=weight_send.at[u, d - 1],
                recv_sem=weight_recv.at[u, other],
                device_id={"chan": other},
                device_id_type=MESH,
            ).wait_recv()

    def enter(u, x):
        hat, inv = unit(x)
        normed = (hat * in_gain_ref[u : u + 1, :]).astype(BF16)
        wide = weight[u].reshape(4 * hid, ch)
        proj_ref[u] = dot_t(normed, wide)
        mask = mask_ref[...].reshape(cells, ch)
        left = jax.nn.sigmoid(proj_ref[u, :, 0:hid]) * proj_ref[u, :, hid : 2 * hid] * mask
        right = (
            jax.nn.sigmoid(proj_ref[u, :, 2 * hid : 3 * hid])
            * proj_ref[u, :, 3 * hid : 4 * hid]
            * mask
        )
        return hat, inv, normed, left, right

    def gate_of(u, normed):
        return jax.nn.sigmoid(dot(normed, gate_proj_ref[u]))

    def product(left_kind, right_kind, left_major, start):
        acc_ref[...] = jnp.zeros_like(acc_ref)

        def body(d, carry):
            s = lax.rem(start + d, n)
            arrive(left_kind, s)
            arrive(right_kind, s)
            lhs_ref[...] = buf[left_kind, s].astype(F32)
            for low in range(0, t, 8):
                acc = acc_ref[low : low + 8]
                for k in range(t):
                    right = buf[right_kind, s, k].astype(F32)
                    if left_major:
                        left = lhs_ref[low : low + 8, k : k + 1, :]
                    else:
                        left = lhs_ref[k, low : low + 8, :].reshape(8, 1, hid)
                    acc = acc + left * right[None]
                acc_ref[low : low + 8] = acc
            return carry

        lax.fori_loop(0, n, body, 0)
        return acc_ref[...].reshape(cells, hid)

    def drop(kind, slot, value):
        buf[kind, slot] = value

    def finish(u, hidden, x, gate):
        hat, inv = unit(hidden)
        scaled = (hat * out_gain_ref[u : u + 1, :]).astype(BF16)
        update = dot(scaled, out_proj_ref[u])
        return hat, inv, update, x + gate * update

    def leave(u, grad, gate, update, hat, inv):
        d_update = grad * gate
        d_logit = d_update * update * (1.0 - gate)
        d_scaled = dot_t(d_update.astype(BF16), out_proj_ref[u])
        d_hidden = unit_back(hat, inv, d_scaled * out_gain_ref[u : u + 1, :])
        return d_hidden, d_logit

    def entry(u, grad, d_left, d_right, d_normed, hat, inv):
        mask = mask_ref[...].reshape(cells, ch)
        for side, value in ((0, d_left * mask), (2, d_right * mask)):
            gate = jax.nn.sigmoid(proj_ref[u, :, side * hid : (side + 1) * hid])
            held = proj_ref[u, :, (side + 1) * hid : (side + 2) * hid]
            slope = value * gate
            wide_ref[:, side * hid : (side + 1) * hid] = (slope * held * (1.0 - gate)).astype(BF16)
            wide_ref[:, (side + 1) * hid : (side + 2) * hid] = slope.astype(BF16)
        d_entry = dot(wide_ref[...], weight[u].reshape(4 * hid, ch))
        return grad + unit_back(hat, inv, (d_entry + d_normed) * in_gain_ref[u : u + 1, :])

    own = pl.ds(pl.multiple_of(chan * t, t), t)
    x0 = pair_ref[:, own, :].astype(F32).reshape(cells, ch)
    wait_weight(0)
    hat0, inv0, normed0, left, right = enter(0, x0)
    turned = jnp.swapaxes(right.reshape(t, t, hid), 0, 1).astype(BF16)
    stage[0] = turned
    pl.when(same)(lambda: drop(B0_TOQ, q, turned))
    push(B0_TOQ, stage.at[0])
    left = left.astype(BF16).reshape(t, t, hid)
    right = right.astype(BF16).reshape(t, t, hid)
    drop(A0_ROW, q, left)
    push(A0_ROW, buf.at[A0_ROW, q])
    gate0 = gate_of(0, normed0)
    hidden0 = product(A0_ROW, B0_TOQ, True, q)
    hidden0 = hidden0.astype(BF16).astype(F32)
    hid0, hid_inv0, update0, middle = finish(0, hidden0, x0, gate0)
    x1 = middle.astype(BF16).astype(F32)

    wait_weight(1)
    hat1, inv1, normed1, left1, right1 = enter(1, x1)
    left1 = left1.astype(BF16).reshape(t, t, hid)
    right1 = right1.astype(BF16).reshape(t, t, hid)
    drop(A1_ROW, q, left1)
    pl.when(same)(lambda: drop(A1_TOR, r, left1))
    push(A1_TOR, buf.at[A1_ROW, q])
    drop(B1_COL, r, right1)
    push(B1_COL, buf.at[B1_COL, r])
    push(A1_ROW, buf.at[A1_ROW, q])
    drop(B1_ROW, q, right1)
    push(B1_ROW, buf.at[B1_ROW, q])
    gate1 = gate_of(1, normed1)
    hidden1 = product(A1_TOR, B1_COL, False, r)
    hidden1 = hidden1.astype(BF16).astype(F32)
    hid1, hid_inv1, update1, final = finish(1, hidden1, x1, gate1)

    grad2 = cot_ref[...].astype(F32).reshape(cells, ch)
    d_hidden, d_logit = leave(1, grad2, gate1, update1, hid1, hid_inv1)
    turned1 = jnp.swapaxes(d_hidden.reshape(t, t, hid), 0, 1).astype(BF16)
    stage[1] = turned1
    pl.when(same)(lambda: drop(D1_TOQ, q, turned1))
    push(D1_TOQ, stage.at[1])
    drop(D1_COL, r, d_hidden.astype(BF16).reshape(t, t, hid))
    push(D1_COL, buf.at[D1_COL, r])
    new_ref[...] = final.astype(BF16).reshape(t, t, ch)
    drop(A0_COL, r, left)
    push(A0_COL, buf.at[A0_COL, r])
    drop(B0_COL, r, right)
    push(B0_COL, buf.at[B0_COL, r])
    d_normed = dot_t(d_logit.astype(BF16), gate_proj_ref[1])
    d_right = product(A1_ROW, D1_COL, True, r)
    d_left = product(B1_ROW, D1_TOQ, True, q)
    grad1 = entry(1, grad2, d_left, d_right, d_normed, hat1, inv1)

    d_hidden, d_logit = leave(0, grad1, gate0, update0, hid0, hid_inv0)
    d_hidden = d_hidden.astype(BF16).reshape(t, t, hid)
    drop(D0_ROW, q, d_hidden)
    pl.when(same)(lambda: drop(D0_TOR, r, d_hidden))
    push(D0_TOR, buf.at[D0_ROW, q])
    push(D0_ROW, buf.at[D0_ROW, q])
    d_normed = dot_t(d_logit.astype(BF16), gate_proj_ref[0])
    d_left = product(D0_ROW, B0_COL, True, q)
    d_right = product(D0_TOR, A0_COL, False, r)
    grad0 = entry(0, grad1, d_left, d_right, d_normed, hat0, inv0)
    grad_ref[...] = grad0.reshape(t, t, ch)

    for copy in weight_copies:
        copy.wait_send()
    for copy, maybe_self in pending:
        if maybe_self:
            pl.when(jnp.logical_not(same))(copy.wait_send)
        else:
            copy.wait_send()


def shards(
    n,
    n_chan,
    pair,
    window_start,
    residue_mask,
    in_gain,
    in_proj,
    gate_proj,
    out_gain,
    out_proj,
    cotangent,
):
    t, half, ch = cotangent.shape
    hid = out_proj.shape[1]
    turned = jnp.transpose(in_proj, (0, 2, 3, 1))
    vmem = pl.BlockSpec(memory_space=pltpu.VMEM)
    smem = pl.BlockSpec(memory_space=pltpu.SMEM)
    return pl.pallas_call(
        functools.partial(kernel, n, n_chan),
        out_shape=(
            jax.ShapeDtypeStruct((t, half, ch), BF16),
            jax.ShapeDtypeStruct((t, half, ch), F32),
        ),
        in_specs=[vmem, smem, smem] + [vmem] * 6,
        out_specs=(vmem, vmem),
        scratch_shapes=[
            pltpu.VMEM((KINDS, n, t, t, hid), BF16),
            pltpu.VMEM((2, t, t, hid), BF16),
            pltpu.VMEM((2, 4, hid, ch), BF16),
            pltpu.VMEM((t, t, ch), F32),
            pltpu.VMEM((t, t, hid), F32),
            pltpu.VMEM((t, t, hid), F32),
            pltpu.VMEM((2, t * t, 4 * hid), F32),
            pltpu.VMEM((t * t, 4 * hid), BF16),
            pltpu.SemaphoreType.DMA((KINDS, n)),
            pltpu.SemaphoreType.DMA((KINDS, n)),
            pltpu.SemaphoreType.DMA((2, n_chan)),
            pltpu.SemaphoreType.DMA((2, n_chan)),
        ],
        compiler_params=pltpu.CompilerParams(
            collective_id=0, has_side_effects=True, vmem_limit_bytes=40 * 1024 * 1024
        ),
    )(pair, window_start, residue_mask, in_gain, turned, gate_proj, out_gain, out_proj, cotangent)


def solution(mesh):
    n = mesh.shape["row"]
    n_chan = mesh.shape["chan"]
    assert n == mesh.shape["col"] * n_chan
    placed = (
        P(("grp", "row"), "col", None),
        P("grp"),
        P("grp"),
        P(),
        P(None, None, None, "chan"),
        P(),
        P(),
        P(),
        P(("grp", "row"), ("col", "chan"), None),
    )
    out = P(("grp", "row"), ("col", "chan"), None)
    return jax.shard_map(
        functools.partial(shards, n, n_chan),
        mesh=mesh,
        in_specs=placed,
        out_specs=(out, out),
        check_vma=False,
    )
```

time: 247 us -> 83.7 us (0.34)
  blocking collectives: 87.5 us -> 0 us
  Pallas kernels: 0 us -> 75.1 us
  waiting for transfers between devices: 57.7 us -> 0 us
  local copies, waits for them, and re-layouts: 39.4 us -> 6.96 us
  other arithmetic: 26.1 us -> 0 us
  matrix products: 18 us -> 0 us
  between operations: 15.9 us -> 1.33 us
    pallas_call x0 -> x1, Pallas kernels: none -> 75.1 us  [shards(): pl.pallas_call(functools.partial(kernel, n, n_chan), out_shape=(jax.Shape...]
    all_gather x7 -> x0, blocking collectives: 64.4 us -> none  [the longest x1 20.5 us: shards(): d_hidden_rows = lax.all_gather(d_hidden_one, 'row', axis=0, tiled=True)]
    reduce_scatter x6 -> x0, waiting for transfers between devices: 57.6 us -> none  [the longest x1 20.3 us: shards(): lax.psum_scatter(jnp.einsum('ijh,hik->jhk', picked, left_zero, preferred_...]
    all_to_all x4 -> x0, blocking collectives: 23.1 us -> none  [the longest x2 15.7 us: split_cells(): lax.all_to_all(hidden, 'chan', split_axis=1, concat_axis=2, tiled=True)]
    dot_general x20 -> x0, matrix products: 18 us -> none  [the longest x4 3.56 us: project_pair(): jnp.einsum('ijc,cgh->ghij', normed, weight, preferred_element_type=jnp.fl...]
    convert_element_type x15 -> x0, local copies, waits for them, and re-layouts: 15 us -> none  [the longest x1 2.89 us: shards(): jnp.einsum('hki,hkj->ijh', picked, right_one, preferred_element_type=jnp....]
    reduce_sum x21 -> x0, other arithmetic: 9.59 us -> none  [the longest x13 5.76 us: layer_norm(): center = values - jnp.mean(values, axis=-1, keepdims=True)]
    convert_element_type x13 -> x0, other arithmetic: 7.61 us -> none  [the longest x2 2.16 us: finish_update(): scaled = layer_norm(hidden, hidden_gain).astype(jnp.bfloat16)]
  transfers between devices with their start and end apart: 6 -> 0, of which waited for: 5 -> 0; matrix products, arithmetic and copies ran while one was open for 8% -> 0% of each run, Pallas kernels for 0% -> 0%
where the time goes in v1:
time: 83.7 us; the launch traced here: 83.3 us
  Pallas kernels  75.1 us (90%)
  local copies, waits for them, and re-layouts  6.96 us (8%)
  between operations  1.33 us (2%)
    pallas_call x1, Pallas kernels, shards(): pl.pallas_call(functools.partial(kernel, n, n_chan), out_shape=(jax.Shape...  75.1 us
    unnamed x18, local copies, waits for them, and re-layouts  6.96 us

profile of v1, /device:TPU:3, one launch (start us, length us, event | category | flops | bytes accessed | tf_op | source)
XLA Modules:
  0.0 83.3 jit_solution(914500159910761316)
XLA Ops:
  0.6 0.0 copy-start.7
  1.3 0.0 copy-start.6
  1.3 0.0 copy-done.7
  1.3 0.7 copy-done.6
  2.0 0.0 copy-start
  2.0 0.9 %copy-done = bf16[16,32,128]{2,1,0:T(8,128)(2,1)S(1)} copy-done((bf16[16,32,128]{2,1,0:T(8,128)(2,1)S(1)}, bf16[16,32,128]{2,1,0:T(8,128)(2,1)}, u32[]{:S(2)}) %copy-start) | copy-done | bytes 131096
  2.9 0.0 copy-start.1
  2.9 0.9 %copy-done.1 = bf16[2,128,4,64]{1,3,2,0:T(8,128)(2,1)S(1)} copy-done((bf16[2,128,4,64]{1,3,2,0:T(8,128)(2,1)S(1)}, bf16[2,128,4,64]{1,3,2,0:T(8,128)(2,1)}, u32[]{:S(2)}) %copy-start.1) | copy-done | bytes 131096
  3.8 0.0 copy-start.2
  3.8 0.8 %copy-done.2 = bf16[2,128,128]{2,1,0:T(8,128)(2,1)S(1)} copy-done((bf16[2,128,128]{2,1,0:T(8,128)(2,1)S(1)}, bf16[2,128,128]{2,1,0:T(8,128)(2,1)}, u32[]{:S(2)}) %copy-start.2) | copy-done | bytes 65560
  4.6 0.0 copy-start.3
  4.6 0.8 %copy-done.3 = bf16[2,128,128]{2,1,0:T(8,128)(2,1)S(1)} copy-done((bf16[2,128,128]{2,1,0:T(8,128)(2,1)S(1)}, bf16[2,128,128]{2,1,0:T(8,128)(2,1)}, u32[]{:S(2)}) %copy-start.3) | copy-done | bytes 65560
  5.5 0.0 copy-start.4
  5.5 0.8 %copy-done.4 = bf16[16,16,128]{2,1,0:T(8,128)(2,1)S(1)} copy-done((bf16[16,16,128]{2,1,0:T(8,128)(2,1)S(1)}, bf16[16,16,128]{2,1,0:T(8,128)(2,1)}, u32[]{:S(2)}) %copy-start.4) | copy-done | bytes 65560
  6.3 0.0 copy-start.5
  6.3 0.7 copy-done.5
  7.0 75.1 %shard_map.104 = (bf16[16,16,128]{2,1,0:T(8,128)(2,1)S(1)}, f32[16,16,128]{2,1,0:T(8,128)S(1)}) custom-call(bf16[16,32,128]{2,1,0:T(8,128)(2,1)S(1)} %copy-done, s32[1]{0:T(128)S(6)} %copy.13.start_ref, s32[1024]{0:T(1024)S(1)} %copy-done.5, f32[2,128]{1,0:T(2,128)S(1)} %copy-done.6, bf16[2,4,64,128]{3,2,1,0:T(8,128)(2,1)S(1)} %bitcast.1, ...), custom_call_target="tpu_custom_call" | custom-call | tf_op jit(solution)/shard_map/pallas_call | solution.py:358
  82.1 0.6 copy.14
  82.7 0.7 copy.15
Async XLA Ops:
  0.6 0.7 copy-start.7
  1.3 0.7 copy-start.6
  2.0 0.9 %copy-start = (bf16[16,32,128]{2,1,0:T(8,128)(2,1)S(1)}, bf16[16,32,128]{2,1,0:T(8,128)(2,1)}, u32[]{:S(2)}) copy-start(bf16[16,32,128]{2,1,0:T(8,128)(2,1)} %pair_ref.1) | copy-start | bytes 393220
  2.9 0.9 %copy-start.1 = (bf16[2,128,4,64]{1,3,2,0:T(8,128)(2,1)S(1)}, bf16[2,128,4,64]{1,3,2,0:T(8,128)(2,1)}, u32[]{:S(2)}) copy-start(bf16[2,128,4,64]{1,3,2,0:T(8,128)(2,1)} %param.13) | copy-start | bytes 393220
  3.8 0.8 %copy-start.2 = (bf16[2,128,128]{2,1,0:T(8,128)(2,1)S(1)}, bf16[2,128,128]{2,1,0:T(8,128)(2,1)}, u32[]{:S(2)}) copy-start(bf16[2,128,128]{2,1,0:T(8,128)(2,1)} %gate_proj_ref.1) | copy-start | bytes 196612
  4.6 0.8 %copy-start.3 = (bf16[2,128,128]{2,1,0:T(8,128)(2,1)S(1)}, bf16[2,128,128]{2,1,0:T(8,128)(2,1)}, u32[]{:S(2)}) copy-start(bf16[2,128,128]{2,1,0:T(8,128)(2,1)} %out_proj_ref.1) | copy-start | bytes 196612
  5.5 0.8 %copy-start.4 = (bf16[16,16,128]{2,1,0:T(8,128)(2,1)S(1)}, bf16[16,16,128]{2,1,0:T(8,128)(2,1)}, u32[]{:S(2)}) copy-start(bf16[16,16,128]{2,1,0:T(8,128)(2,1)} %cot_ref.1) | copy-start | bytes 196612
  6.3 0.7 copy-start.5

commit v2 on v1

--- a/solution.py
+++ b/solution.py
@@ -11,9 +11,9 @@
 BF16 = jnp.bfloat16
 MESH = pl.DeviceIdType.MESH
 
-A0_ROW, B0_TOQ, A0_COL, B0_COL, B1_COL, A1_TOR, A1_ROW, B1_ROW = range(8)
-D1_COL, D1_TOQ, D0_ROW, D0_TOR = range(8, 12)
-KINDS = 12
+B0, A1, D1, D0, H0, H1, L1, R0 = range(8)
+KINDS = 8
+IN_ROW = (A1, D0, H0, L1)
 
 
 def dot(a, b):
@@ -56,6 +56,7 @@
     mask_ref,
     lhs_ref,
     acc_ref,
+    local,
     proj_ref,
     wide_ref,
     send_sem,
@@ -70,92 +71,54 @@
     r = lax.axis_index("row")
     chan = lax.axis_index("chan")
     q = lax.axis_index("col") * n_chan + chan
-    same = r == q
-
-    def at(row, place):
-        return {"row": row, "col": place // n_chan, "chan": lax.rem(place, n_chan)}
-
-    def targets(way):
-        if way == "row":
-            return [(at(r, lax.rem(q + d, n)), False) for d in range(1, n)]
-        if way == "col":
-            return [(at(lax.rem(r + d, n), q), False) for d in range(1, n)]
-        if way == "to_q":
-            return [(at(lax.rem(r + d, n), r), d == 0) for d in range(n)]
-        return [(at(q, lax.rem(q + d, n)), d == 0) for d in range(n)]
-
-    ways = {
-        A0_ROW: "row",
-        A1_ROW: "row",
-        B1_ROW: "row",
-        D0_ROW: "row",
-        A0_COL: "col",
-        B0_COL: "col",
-        B1_COL: "col",
-        D1_COL: "col",
-        B0_TOQ: "to_q",
-        D1_TOQ: "to_q",
-        A1_TOR: "to_r",
-        D0_TOR: "to_r",
-    }
+
+    def peer(in_row, place):
+        if in_row:
+            return {"col": place // n_chan, "chan": lax.rem(place, n_chan)}
+        return {"row": place}
+
+    def here(kind):
+        return q if kind in IN_ROW else r
+
+    def after(place, d):
+        return lax.rem(place + d, n)
 
     barrier = pltpu.get_barrier_semaphore()
-    for way in ("row", "col", "to_q", "to_r"):
-        for device, maybe_self in targets(way):
-
-            def greet(device=device):
-                pl.semaphore_signal(barrier, inc=1, device_id=device, device_id_type=MESH)
-
-            if maybe_self:
-                pl.when(jnp.logical_not(same))(greet)
-            else:
-                greet()
-    count = 4 * n - 2
-
-    @pl.when(same)
-    def _():
-        pl.semaphore_wait(barrier, count - 2)
-
-    @pl.when(jnp.logical_not(same))
-    def _():
-        pl.semaphore_wait(barrier, count)
-
-    def slot_of(kind):
-        return q if ways[kind] in ("row", "to_q") else r
-
-    pending = []
-
-    def push(kind, source):
-        slot = slot_of(kind)
-        for step, (device, maybe_self) in enumerate(targets(ways[kind])):
-            copy = pltpu.make_async_remote_copy(
-                src_ref=source,
-                dst_ref=buf.at[kind, slot],
-                send_sem=send_sem.at[kind, step],
-                recv_sem=recv_sem.at[kind, slot],
-                device_id=device,
+    for in_row in (True, False):
+        for d in range(1, n):
+            pl.semaphore_signal(
+                barrier,
+                inc=1,
+                device_id=peer(in_row, after(q if in_row else r, d)),
                 device_id_type=MESH,
             )
-            pending.append((copy, maybe_self))
-            if maybe_self:
-                pl.when(jnp.logical_not(same))(copy.start)
-            else:
-                copy.start()
+    pl.semaphore_wait(barrier, 2 * (n - 1))
+
+    def move(kind, place, source):
+        return pltpu.make_async_remote_copy(
+            src_ref=source,
+            dst_ref=buf.at[kind, here(kind)],
+            send_sem=send_sem.at[kind, place],
+            recv_sem=recv_sem.at[kind, here(kind)],
+            device_id=peer(kind in IN_ROW, place),
+            device_id_type=MESH,
+        )
+
+    def share(kind, value):
+        buf[kind, here(kind)] = value
+        for d in range(1, n):
+            move(kind, after(here(kind), d), buf.at[kind, here(kind)]).start()
 
     def arrive(kind, slot):
         copy = pltpu.make_async_remote_copy(
             src_ref=buf.at[kind, slot],
             dst_ref=buf.at[kind, slot],
-            send_sem=send_sem.at[kind, 0],
+            send_sem=send_sem.at[kind, slot],
             recv_sem=recv_sem.at[kind, slot],
-            device_id={"row": r},
+            device_id=peer(kind in IN_ROW, slot),
             device_id_type=MESH,
         )
-        way = ways[kind]
-        if way in ("row", "col"):
-            pl.when(slot != (q if way == "row" else r))(copy.wait_recv)
-        else:
-            pl.when(jnp.logical_not(jnp.logical_and(same, slot == r)))(copy.wait_recv)
+        pl.when(slot != here(kind))(copy.wait_recv)
 
     part = in_proj_ref.shape[2]
     mine = pl.ds(pl.multiple_of(chan * part, part), part)
@@ -213,31 +176,64 @@
     def gate_of(u, normed):
         return jax.nn.sigmoid(dot(normed, gate_proj_ref[u]))
 
-    def product(left_kind, right_kind, left_major, start):
+    def multiply(left_major, right_of):
+        for low in range(0, t, 8):
+            acc = acc_ref[low : low + 8]
+            for k in range(t):
+                if left_major:
+                    left = lhs_ref[low : low + 8, k : k + 1, :]
+                else:
+                    left = lhs_ref[k, low : low + 8, :].reshape(8, 1, hid)
+                acc = acc + left * right_of(k)[None]
+            acc_ref[low : low + 8] = acc
+
+    def product(left_kind, right_kind):
         acc_ref[...] = jnp.zeros_like(acc_ref)
 
-        def body(d, carry):
-            s = lax.rem(start + d, n)
-            arrive(left_kind, s)
-            arrive(right_kind, s)
+        def body(s, carry):
             lhs_ref[...] = buf[left_kind, s].astype(F32)
-            for low in range(0, t, 8):
-                acc = acc_ref[low : low + 8]
-                for k in range(t):
-                    right = buf[right_kind, s, k].astype(F32)
-                    if left_major:
-                        left = lhs_ref[low : low + 8, k : k + 1, :]
-                    else:
-                        left = lhs_ref[k, low : low + 8, :].reshape(8, 1, hid)
-                    acc = acc + left * right[None]
-                acc_ref[low : low + 8] = acc
+            multiply(True, lambda k: buf[right_kind, s, k].astype(F32))
             return carry
 
         lax.fori_loop(0, n, body, 0)
         return acc_ref[...].reshape(cells, hid)
 
-    def drop(kind, slot, value):
-        buf[kind, slot] = value
+    def partials(kind, out_kind, left_major):
+        def body(d, carry):
+            s = after(here(kind), n - d)
+            arrive(kind, s)
+            lhs_ref[...] = buf[kind, s].astype(F32)
+            acc_ref[...] = jnp.zeros_like(acc_ref)
+            multiply(left_major, lambda k: local[k])
+            out = stage.at[out_kind - H0, s]
+            out[...] = acc_ref[...].astype(BF16)
+
+            @pl.when(s != here(out_kind))
+            def _():
+                move(out_kind, s, out).start()
+
+            @pl.when(s == here(out_kind))
+            def _():
+                buf[out_kind, s] = acc_ref[...].astype(BF16)
+
+            return carry
+
+        lax.fori_loop(0, n, body, 0)
+
+    def total(kind):
+        acc_ref[...] = jnp.zeros_like(acc_ref)
+
+        def body(d, carry):
+            s = after(here(kind), n - d)
+            arrive(kind, s)
+            acc_ref[...] += buf[kind, s].astype(F32)
+            return carry
+
+        lax.fori_loop(0, n, body, 0)
+        return acc_ref[...]
+
+    def turn(value):
+        return jnp.swapaxes(value.reshape(t, t, hid), 0, 1)
 
     def finish(u, hidden, x, gate):
         hat, inv = unit(hidden)
@@ -267,74 +263,51 @@
     x0 = pair_ref[:, own, :].astype(F32).reshape(cells, ch)
     wait_weight(0)
     hat0, inv0, normed0, left, right = enter(0, x0)
-    turned = jnp.swapaxes(right.reshape(t, t, hid), 0, 1).astype(BF16)
-    stage[0] = turned
-    pl.when(same)(lambda: drop(B0_TOQ, q, turned))
-    push(B0_TOQ, stage.at[0])
-    left = left.astype(BF16).reshape(t, t, hid)
-    right = right.astype(BF16).reshape(t, t, hid)
-    drop(A0_ROW, q, left)
-    push(A0_ROW, buf.at[A0_ROW, q])
+    share(B0, right.astype(BF16).reshape(t, t, hid))
+    left0 = left.astype(BF16).astype(F32).reshape(t, t, hid)
+    local[...] = turn(left0)
     gate0 = gate_of(0, normed0)
-    hidden0 = product(A0_ROW, B0_TOQ, True, q)
-    hidden0 = hidden0.astype(BF16).astype(F32)
+    partials(B0, H0, True)
+    hidden0 = turn(total(H0)).reshape(cells, hid).astype(BF16).astype(F32)
     hid0, hid_inv0, update0, middle = finish(0, hidden0, x0, gate0)
     x1 = middle.astype(BF16).astype(F32)
 
     wait_weight(1)
-    hat1, inv1, normed1, left1, right1 = enter(1, x1)
-    left1 = left1.astype(BF16).reshape(t, t, hid)
-    right1 = right1.astype(BF16).reshape(t, t, hid)
-    drop(A1_ROW, q, left1)
-    pl.when(same)(lambda: drop(A1_TOR, r, left1))
-    push(A1_TOR, buf.at[A1_ROW, q])
-    drop(B1_COL, r, right1)
-    push(B1_COL, buf.at[B1_COL, r])
-    push(A1_ROW, buf.at[A1_ROW, q])
-    drop(B1_ROW, q, right1)
-    push(B1_ROW, buf.at[B1_ROW, q])
+    hat1, inv1, normed1, left, right = enter(1, x1)
+    share(A1, left.astype(BF16).reshape(t, t, hid))
+    right1 = right.astype(BF16).astype(F32).reshape(t, t, hid)
+    local[...] = right1
     gate1 = gate_of(1, normed1)
-    hidden1 = product(A1_TOR, B1_COL, False, r)
-    hidden1 = hidden1.astype(BF16).astype(F32)
+    partials(A1, H1, False)
+    local[...] = turn(right1)
+    hidden1 = total(H1).reshape(cells, hid).astype(BF16).astype(F32)
     hid1, hid_inv1, update1, final = finish(1, hidden1, x1, gate1)
 
     grad2 = cot_ref[...].astype(F32).reshape(cells, ch)
     d_hidden, d_logit = leave(1, grad2, gate1, update1, hid1, hid_inv1)
-    turned1 = jnp.swapaxes(d_hidden.reshape(t, t, hid), 0, 1).astype(BF16)
-    stage[1] = turned1
-    pl.when(same)(lambda: drop(D1_TOQ, q, turned1))
-    push(D1_TOQ, stage.at[1])
-    drop(D1_COL, r, d_hidden.astype(BF16).reshape(t, t, hid))
-    push(D1_COL, buf.at[D1_COL, r])
+    share(D1, d_hidden.astype(BF16).reshape(t, t, hid))
     new_ref[...] = final.astype(BF16).reshape(t, t, ch)
-    drop(A0_COL, r, left)
-    push(A0_COL, buf.at[A0_COL, r])
-    drop(B0_COL, r, right)
-    push(B0_COL, buf.at[B0_COL, r])
     d_normed = dot_t(d_logit.astype(BF16), gate_proj_ref[1])
-    d_right = product(A1_ROW, D1_COL, True, r)
-    d_left = product(B1_ROW, D1_TOQ, True, q)
+    partials(D1, L1, True)
+    d_right = product(A1, D1)
+    d_left = turn(total(L1)).reshape(cells, hid)
     grad1 = entry(1, grad2, d_left, d_right, d_normed, hat1, inv1)
 
     d_hidden, d_logit = leave(0, grad1, gate0, update0, hid0, hid_inv0)
-    d_hidden = d_hidden.astype(BF16).reshape(t, t, hid)
-    drop(D0_ROW, q, d_hidden)
-    pl.when(same)(lambda: drop(D0_TOR, r, d_hidden))
-    push(D0_TOR, buf.at[D0_ROW, q])
-    push(D0_ROW, buf.at[D0_ROW, q])
+    share(D0, d_hidden.astype(BF16).reshape(t, t, hid))
+    local[...] = left0
     d_normed = dot_t(d_logit.astype(BF16), gate_proj_ref[0])
-    d_left = product(D0_ROW, B0_COL, True, q)
-    d_right = product(D0_TOR, A0_COL, False, r)
+    partials(D0, R0, False)
+    d_left = product(D0, B0)
+    d_right = total(R0).reshape(cells, hid)
     grad0 = entry(0, grad1, d_left, d_right, d_normed, hat0, inv0)
     grad_ref[...] = grad0.reshape(t, t, ch)
 
     for copy in weight_copies:
         copy.wait_send()
-    for copy, maybe_self in pending:
-        if maybe_self:
-            pl.when(jnp.logical_not(same))(copy.wait_send)
-        else:
-            copy.wait_send()
+    for kind in range(KINDS):
+        for d in range(1, n):
+            move(kind, after(here(kind), d), buf.at[kind, here(kind)]).wait_send()
 
 
 def shards(
@@ -365,9 +338,10 @@
         out_specs=(vmem, vmem),
         scratch_shapes=[
             pltpu.VMEM((KINDS, n, t, t, hid), BF16),
-            pltpu.VMEM((2, t, t, hid), BF16),
+            pltpu.VMEM((KINDS - H0, n, t, t, hid), BF16),
             pltpu.VMEM((2, 4, hid, ch), BF16),
             pltpu.VMEM((t, t, ch), F32),
+            pltpu.VMEM((t, t, hid), F32),
             pltpu.VMEM((t, t, hid), F32),
             pltpu.VMEM((t, t, hid), F32),
             pltpu.VMEM((2, t * t, 4 * hid), F32),

time: 83.7 us -> 57.6 us (0.69)
  Pallas kernels: 75.1 us -> 49 us
    pallas_call x1, Pallas kernels: 75.1 us -> 49 us  [shards(): pl.pallas_call(functools.partial(kernel, n, n_chan), out_shape=(jax.Shape...]
where the time goes in v2:
time: 57.6 us; the launch traced here: 57.3 us
  Pallas kernels  49 us (85%)
  local copies, waits for them, and re-layouts  6.96 us (12%)
  between operations  1.33 us (2%)
    pallas_call x1, Pallas kernels, shards(): pl.pallas_call(functools.partial(kernel, n, n_chan), out_shape=(jax.Shape...  49 us
    unnamed x18, local copies, waits for them, and re-layouts  6.96 us

profile of v2, /device:TPU:3, one launch (start us, length us, event | category | flops | bytes accessed | tf_op | source)
XLA Modules:
  0.0 57.3 jit_solution(5187949321109385215)
XLA Ops:
  0.6 0.0 copy-start.7
  1.3 0.0 copy-start.6
  1.3 0.0 copy-done.7
  1.3 0.7 %copy-done.6 = f32[2,128]{1,0:T(2,128)S(1)} copy-done((f32[2,128]{1,0:T(2,128)S(1)}, f32[2,128]{1,0:T(2,128)}, u32[]{:S(2)}) %copy-start.6) | copy-done | bytes 1048
  2.0 0.0 copy-start
  2.0 0.9 %copy-done = bf16[16,32,128]{2,1,0:T(8,128)(2,1)S(1)} copy-done((bf16[16,32,128]{2,1,0:T(8,128)(2,1)S(1)}, bf16[16,32,128]{2,1,0:T(8,128)(2,1)}, u32[]{:S(2)}) %copy-start) | copy-done | bytes 131096
  2.9 0.0 copy-start.1
  2.9 0.9 %copy-done.1 = bf16[2,128,4,64]{1,3,2,0:T(8,128)(2,1)S(1)} copy-done((bf16[2,128,4,64]{1,3,2,0:T(8,128)(2,1)S(1)}, bf16[2,128,4,64]{1,3,2,0:T(8,128)(2,1)}, u32[]{:S(2)}) %copy-start.1) | copy-done | bytes 131096
  3.8 0.0 copy-start.2
  3.8 0.8 %copy-done.2 = bf16[2,128,128]{2,1,0:T(8,128)(2,1)S(1)} copy-done((bf16[2,128,128]{2,1,0:T(8,128)(2,1)S(1)}, bf16[2,128,128]{2,1,0:T(8,128)(2,1)}, u32[]{:S(2)}) %copy-start.2) | copy-done | bytes 65560
  4.6 0.0 copy-start.3
  4.6 0.8 %copy-done.3 = bf16[2,128,128]{2,1,0:T(8,128)(2,1)S(1)} copy-done((bf16[2,128,128]{2,1,0:T(8,128)(2,1)S(1)}, bf16[2,128,128]{2,1,0:T(8,128)(2,1)}, u32[]{:S(2)}) %copy-start.3) | copy-done | bytes 65560
  5.5 0.0 copy-start.4
  5.5 0.8 %copy-done.4 = bf16[16,16,128]{2,1,0:T(8,128)(2,1)S(1)} copy-done((bf16[16,16,128]{2,1,0:T(8,128)(2,1)S(1)}, bf16[16,16,128]{2,1,0:T(8,128)(2,1)}, u32[]{:S(2)}) %copy-start.4) | copy-done | bytes 65560
  6.3 0.0 copy-start.5
  6.3 0.7 %copy-done.5 = s32[1024]{0:T(1024)S(1)} copy-done((s32[1024]{0:T(1024)S(1)}, s32[1024]{0:T(1024)}, u32[]{:S(2)}) %copy-start.5) | copy-done | bytes 4120
  7.0 49.0 %shard_map.104 = (bf16[16,16,128]{2,1,0:T(8,128)(2,1)S(1)}, f32[16,16,128]{2,1,0:T(8,128)S(1)}) custom-call(bf16[16,32,128]{2,1,0:T(8,128)(2,1)S(1)} %copy-done, s32[1]{0:T(128)S(6)} %copy.13.start_ref, s32[1024]{0:T(1024)S(1)} %copy-done.5, f32[2,128]{1,0:T(2,128)S(1)} %copy-done.6, bf16[2,4,64,128]{3,2,1,0:T(8,128)(2,1)S(1)} %bitcast.1, ...), custom_call_target="tpu_custom_call" | custom-call | tf_op jit(solution)/shard_map/pallas_call | solution.py:331
  56.0 0.6 %copy.14 = bf16[16,16,128]{2,1,0:T(8,128)(2,1)} copy(bf16[16,16,128]{2,1,0:T(8,128)(2,1)S(1)} %get-tuple-element.4) | data formatting | bytes 131072
  56.6 0.7 %copy.15 = f32[16,16,128]{2,1,0:T(8,128)} copy(f32[16,16,128]{2,1,0:T(8,128)S(1)} %get-tuple-element.5) | data formatting | bytes 262144
Async XLA Ops:
  0.6 0.7 %copy-start.7 = (f32[2,128]{1,0:T(2,128)S(1)}, f32[2,128]{1,0:T(2,128)}, u32[]{:S(2)}) copy-start(f32[2,128]{1,0:T(2,128)} %out_gain_ref.1) | copy-start | bytes 3076
  1.3 0.7 %copy-start.6 = (f32[2,128]{1,0:T(2,128)S(1)}, f32[2,128]{1,0:T(2,128)}, u32[]{:S(2)}) copy-start(f32[2,128]{1,0:T(2,128)} %in_gain_ref.1) | copy-start | bytes 3076
  2.0 0.9 %copy-start = (bf16[16,32,128]{2,1,0:T(8,128)(2,1)S(1)}, bf16[16,32,128]{2,1,0:T(8,128)(2,1)}, u32[]{:S(2)}) copy-start(bf16[16,32,128]{2,1,0:T(8,128)(2,1)} %pair_ref.1) | copy-start | bytes 393220
  2.9 0.9 %copy-start.1 = (bf16[2,128,4,64]{1,3,2,0:T(8,128)(2,1)S(1)}, bf16[2,128,4,64]{1,3,2,0:T(8,128)(2,1)}, u32[]{:S(2)}) copy-start(bf16[2,128,4,64]{1,3,2,0:T(8,128)(2,1)} %param.13) | copy-start | bytes 393220
  3.8 0.8 %copy-start.2 = (bf16[2,128,128]{2,1,0:T(8,128)(2,1)S(1)}, bf16[2,128,128]{2,1,0:T(8,128)(2,1)}, u32[]{:S(2)}) copy-start(bf16[2,128,128]{2,1,0:T(8,128)(2,1)} %gate_proj_ref.1) | copy-start | bytes 196612
  4.6 0.8 %copy-start.3 = (bf16[2,128,128]{2,1,0:T(8,128)(2,1)S(1)}, bf16[2,128,128]{2,1,0:T(8,128)(2,1)}, u32[]{:S(2)}) copy-start(bf16[2,128,128]{2,1,0:T(8,128)(2,1)} %out_proj_ref.1) | copy-start | bytes 196612
  5.5 0.8 %copy-start.4 = (bf16[16,16,128]{2,1,0:T(8,128)(2,1)S(1)}, bf16[16,16,128]{2,1,0:T(8,128)(2,1)}, u32[]{:S(2)}) copy-start(bf16[16,16,128]{2,1,0:T(8,128)(2,1)} %cot_ref.1) | copy-start | bytes 196612
  6.3 0.7 %copy-start.5 = (s32[1024]{0:T(1024)S(1)}, s32[1024]{0:T(1024)}, u32[]{:S(2)}) copy-start(s32[1024]{0:T(1024)} %residue_ref.1) | copy-start | bytes 12292

commit v3 on v2

--- a/solution.py
+++ b/solution.py
@@ -39,17 +39,28 @@
 def kernel(
     n,
     n_chan,
+    pair_hbm,
+    start_ref,
+    residue_hbm,
+    in_gain_hbm,
+    in_proj_ref,
+    gate_proj_hbm,
+    out_gain_hbm,
+    out_proj_hbm,
+    cot_hbm,
+    new_hbm,
+    grad_hbm,
+    new_ref,
+    grad_ref,
     pair_ref,
-    start_ref,
     residue_ref,
     in_gain_ref,
-    in_proj_ref,
     gate_proj_ref,
     out_gain_ref,
     out_proj_ref,
     cot_ref,
-    new_ref,
-    grad_ref,
+    load_sem,
+    out_sem,
     buf,
     stage,
     weight,
@@ -64,8 +75,8 @@
     weight_send,
     weight_recv,
 ):
-    t = pair_ref.shape[0]
-    ch = pair_ref.shape[2]
+    t = cot_ref.shape[0]
+    ch = cot_ref.shape[2]
     hid = weight.shape[2]
     cells = t * t
     r = lax.axis_index("row")
@@ -82,6 +93,27 @@
 
     def after(place, d):
         return lax.rem(place + d, n)
+
+    part = in_proj_ref.shape[2]
+    mine = pl.ds(pl.multiple_of(chan * part, part), part)
+    own = pl.ds(pl.multiple_of(chan * t, t), t)
+    loads = [
+        pltpu.make_async_copy(source, target, load_sem.at[place])
+        for place, (source, target) in enumerate(
+            (
+                (pair_hbm.at[:, own, :], pair_ref),
+                (in_proj_ref, weight.at[:, :, mine, :]),
+                (in_gain_hbm, in_gain_ref),
+                (residue_hbm, residue_ref),
+                (gate_proj_hbm, gate_proj_ref),
+                (out_gain_hbm, out_gain_ref),
+                (out_proj_hbm, out_proj_ref),
+                (cot_hbm, cot_ref),
+            )
+        )
+    ]
+    for load in loads:
+        load.start()
 
     barrier = pltpu.get_barrier_semaphore()
     for in_row in (True, False):
@@ -120,8 +152,6 @@
         )
         pl.when(slot != here(kind))(copy.wait_recv)
 
-    part = in_proj_ref.shape[2]
-    mine = pl.ds(pl.multiple_of(chan * part, part), part)
     weight_copies = []
     for u in range(2):
         for d in range(1, n_chan):
@@ -135,7 +165,8 @@
             )
             copy.start()
             weight_copies.append(copy)
-    weight[:, :, mine, :] = in_proj_ref[...]
+    for load in loads:
+        load.wait()
 
     first = start_ref[0]
     rows = lax.broadcasted_iota(jnp.int32, (t, ch), 0)
@@ -161,17 +192,15 @@
 
     def enter(u, x):
         hat, inv = unit(x)
-        normed = (hat * in_gain_ref[u : u + 1, :]).astype(BF16)
-        wide = weight[u].reshape(4 * hid, ch)
-        proj_ref[u] = dot_t(normed, wide)
+        return hat, inv, (hat * in_gain_ref[u : u + 1, :]).astype(BF16)
+
+    def gated(u, normed, side):
+        low, middle, high = side * hid, (side + 1) * hid, (side + 2) * hid
+        wide = weight[u, side : side + 2].reshape(2 * hid, ch)
+        proj_ref[u, :, low:high] = dot_t(normed, wide)
         mask = mask_ref[...].reshape(cells, ch)
-        left = jax.nn.sigmoid(proj_ref[u, :, 0:hid]) * proj_ref[u, :, hid : 2 * hid] * mask
-        right = (
-            jax.nn.sigmoid(proj_ref[u, :, 2 * hid : 3 * hid])
-            * proj_ref[u, :, 3 * hid : 4 * hid]
-            * mask
-        )
-        return hat, inv, normed, left, right
+        value = jax.nn.sigmoid(proj_ref[u, :, low:middle]) * proj_ref[u, :, middle:high] * mask
+        return value.astype(BF16).reshape(t, t, hid)
 
     def gate_of(u, normed):
         return jax.nn.sigmoid(dot(normed, gate_proj_ref[u]))
@@ -259,12 +288,11 @@
         d_entry = dot(wide_ref[...], weight[u].reshape(4 * hid, ch))
         return grad + unit_back(hat, inv, (d_entry + d_normed) * in_gain_ref[u : u + 1, :])
 
-    own = pl.ds(pl.multiple_of(chan * t, t), t)
-    x0 = pair_ref[:, own, :].astype(F32).reshape(cells, ch)
+    x0 = pair_ref[...].astype(F32).reshape(cells, ch)
+    hat0, inv0, normed0 = enter(0, x0)
     wait_weight(0)
-    hat0, inv0, normed0, left, right = enter(0, x0)
-    share(B0, right.astype(BF16).reshape(t, t, hid))
-    left0 = left.astype(BF16).astype(F32).reshape(t, t, hid)
+    share(B0, gated(0, normed0, 2))
+    left0 = gated(0, normed0, 0).astype(F32)
     local[...] = turn(left0)
     gate0 = gate_of(0, normed0)
     partials(B0, H0, True)
@@ -272,10 +300,10 @@
     hid0, hid_inv0, update0, middle = finish(0, hidden0, x0, gate0)
     x1 = middle.astype(BF16).astype(F32)
 
+    hat1, inv1, normed1 = enter(1, x1)
     wait_weight(1)
-    hat1, inv1, normed1, left, right = enter(1, x1)
-    share(A1, left.astype(BF16).reshape(t, t, hid))
-    right1 = right.astype(BF16).astype(F32).reshape(t, t, hid)
+    share(A1, gated(1, normed1, 0))
+    right1 = gated(1, normed1, 2).astype(F32)
     local[...] = right1
     gate1 = gate_of(1, normed1)
     partials(A1, H1, False)
@@ -287,6 +315,8 @@
     d_hidden, d_logit = leave(1, grad2, gate1, update1, hid1, hid_inv1)
     share(D1, d_hidden.astype(BF16).reshape(t, t, hid))
     new_ref[...] = final.astype(BF16).reshape(t, t, ch)
+    new_out = pltpu.make_async_copy(new_ref, new_hbm, out_sem.at[0])
+    new_out.start()
     d_normed = dot_t(d_logit.astype(BF16), gate_proj_ref[1])
     partials(D1, L1, True)
     d_right = product(A1, D1)
@@ -302,12 +332,16 @@
     d_right = total(R0).reshape(cells, hid)
     grad0 = entry(0, grad1, d_left, d_right, d_normed, hat0, inv0)
     grad_ref[...] = grad0.reshape(t, t, ch)
+    grad_out = pltpu.make_async_copy(grad_ref, grad_hbm, out_sem.at[1])
+    grad_out.start()
 
     for copy in weight_copies:
         copy.wait_send()
+    new_out.wait()
     for kind in range(KINDS):
         for d in range(1, n):
             move(kind, after(here(kind), d), buf.at[kind, here(kind)]).wait_send()
+    grad_out.wait()
 
 
 def shards(
@@ -326,7 +360,7 @@
     t, half, ch = cotangent.shape
     hid = out_proj.shape[1]
     turned = jnp.transpose(in_proj, (0, 2, 3, 1))
-    vmem = pl.BlockSpec(memory_space=pltpu.VMEM)
+    hbm = pl.BlockSpec(memory_space=pltpu.HBM)
     smem = pl.BlockSpec(memory_space=pltpu.SMEM)
     return pl.pallas_call(
         functools.partial(kernel, n, n_chan),
@@ -334,9 +368,20 @@
             jax.ShapeDtypeStruct((t, half, ch), BF16),
             jax.ShapeDtypeStruct((t, half, ch), F32),
         ),
-        in_specs=[vmem, smem, smem] + [vmem] * 6,
-        out_specs=(vmem, vmem),
+        in_specs=[hbm, smem] + [hbm] * 7,
+        out_specs=(hbm, hbm),
         scratch_shapes=[
+            pltpu.VMEM((t, half, ch), BF16),
+            pltpu.VMEM((t, half, ch), F32),
+            pltpu.VMEM((t, half, ch), BF16),
+            pltpu.SMEM(residue_mask.shape, jnp.int32),
+            pltpu.VMEM(in_gain.shape, F32),
+            pltpu.VMEM(gate_proj.shape, BF16),
+            pltpu.VMEM(out_gain.shape, F32),
+            pltpu.VMEM(out_proj.shape, BF16),
+            pltpu.VMEM((t, half, ch), BF16),
+            pltpu.SemaphoreType.DMA((8,)),
+            pltpu.SemaphoreType.DMA((2,)),
             pltpu.VMEM((KINDS, n, t, t, hid), BF16),
             pltpu.VMEM((KINDS - H0, n, t, t, hid), BF16),
             pltpu.VMEM((2, 4, hid, ch), BF16),
@@ -352,7 +397,7 @@
             pltpu.SemaphoreType.DMA((2, n_chan)),
         ],
         compiler_params=pltpu.CompilerParams(
-            collective_id=0, has_side_effects=True, vmem_limit_bytes=40 * 1024 * 1024
+            collective_id=0, has_side_effects=True, vmem_limit_bytes=64 * 1024 * 1024
         ),
     )(pair, window_start, residue_mask, in_gain, turned, gate_proj, out_gain, out_proj, cotangent)
 

time: 57.6 us -> 52.7 us (0.915)
  local copies, waits for them, and re-layouts: 6.96 us -> 2.17 us
    unnamed x18 -> x4, local copies, waits for them, and re-layouts: 6.96 us -> 2.17 us
where the time goes in v3:
time: 52.7 us; the launch traced here: 52.5 us
  Pallas kernels  49.1 us (93%)
  local copies, waits for them, and re-layouts  2.17 us (4%)
  between operations  1.29 us (2%)
    pallas_call x1, Pallas kernels, shards(): pl.pallas_call(functools.partial(kernel, n, n_chan), out_shape=(jax.Shape...  49.1 us
    unnamed x4, local copies, waits for them, and re-layouts  2.17 us

profile of v3, /device:TPU:3, one launch (start us, length us, event | category | flops | bytes accessed | tf_op | source)
XLA Modules:
  0.0 52.5 jit_solution(6438737126176522042)
XLA Ops:
  1.3 49.1 %shard_map.104 = (bf16[16,16,128]{2,1,0:T(8,128)(2,1)}, f32[16,16,128]{2,1,0:T(8,128)}) custom-call(bf16[16,32,128]{2,1,0:T(8,128)(2,1)} %pair_hbm.1, s32[1]{0:T(128)S(6)} %copy.13.start_ref, s32[1024]{0:T(1024)} %residue_hbm.1, f32[2,128]{1,0:T(2,128)} %in_gain_hbm.1, bf16[2,4,64,128]{3,2,1,0:T(8,128)(2,1)} %bitcast.1, bf16[2,128,128]{2,1,0:T(8,128)(2,1)} %gate_proj_hbm.1, ...), custom_call_target="tpu_custom_call" | custom-call | tf_op jit(solution)/shard_map/pallas_call | solution.py:365
  50.4 0.0 copy-start
  50.4 1.5 %copy.14 = bf16[16,16,128]{2,1,0:T(8,128)(2,1)} copy(bf16[16,16,128]{2,1,0:T(8,128)(2,1)} %get-tuple-element.4) | data formatting | bytes 131072
  51.9 0.0 copy-done
  51.9 0.7 %copy.15 = f32[16,16,128]{2,1,0:T(8,128)} copy(f32[16,16,128]{2,1,0:T(8,128)S(1)} %copy-done) | data formatting | bytes 262144
Async XLA Ops:
  50.4 1.5 %copy-start = (f32[16,16,128]{2,1,0:T(8,128)S(1)}, f32[16,16,128]{2,1,0:T(8,128)}, u32[]{:S(2)}) copy-start(f32[16,16,128]{2,1,0:T(8,128)} %get-tuple-element.5) | copy-start | bytes 393220

commit v4 on v3

--- a/solution.py
+++ b/solution.py
@@ -11,8 +11,8 @@
 BF16 = jnp.bfloat16
 MESH = pl.DeviceIdType.MESH
 
-B0, A1, D1, D0, H0, H1, L1, R0 = range(8)
-KINDS = 8
+B0, A1, D1, D0, H0, H1, L1, R0, PAIR = range(9)
+KINDS = 9
 IN_ROW = (A1, D0, H0, L1)
 
 
@@ -65,6 +65,7 @@
     stage,
     weight,
     mask_ref,
+    mask_other,
     lhs_ref,
     acc_ref,
     local,
@@ -152,11 +153,12 @@
         )
         pl.when(slot != here(kind))(copy.wait_recv)
 
+    loads[1].wait()
     weight_copies = []
     for u in range(2):
         for d in range(1, n_chan):
             copy = pltpu.make_async_remote_copy(
-                src_ref=in_proj_ref.at[u],
+                src_ref=weight.at[u, :, mine, :],
                 dst_ref=weight.at[u, :, mine, :],
                 send_sem=weight_send.at[u, d - 1],
                 recv_sem=weight_recv.at[u, chan],
@@ -165,7 +167,10 @@
             )
             copy.start()
             weight_copies.append(copy)
-    for load in loads:
+    loads[0].wait()
+    for d in range(1, n):
+        move(PAIR, after(r, d), pair_ref).start()
+    for load in loads[2:]:
         load.wait()
 
     first = start_ref[0]
@@ -182,7 +187,7 @@
             other = lax.rem(chan + d, n_chan)
             theirs = pl.ds(pl.multiple_of(other * part, part), part)
             pltpu.make_async_remote_copy(
-                src_ref=in_proj_ref.at[u],
+                src_ref=weight.at[u, :, theirs, :],
                 dst_ref=weight.at[u, :, theirs, :],
                 send_sem=weight_send.at[u, d - 1],
                 recv_sem=weight_recv.at[u, other],
@@ -201,6 +206,18 @@
         mask = mask_ref[...].reshape(cells, ch)
         value = jax.nn.sigmoid(proj_ref[u, :, low:middle]) * proj_ref[u, :, middle:high] * mask
         return value.astype(BF16).reshape(t, t, hid)
+
+    def project_other(kind, s):
+        @pl.when(s != r)
+        def _():
+            arrive(PAIR, s)
+            normed = enter(0, buf[PAIR, s].astype(F32).reshape(cells, ch))[2]
+            both = dot_t(normed, weight[0, 2:4].reshape(2 * hid, ch))
+            for i in range(t):
+                mask_other[i] = col_mask * residue_ref[first + s * t + i].astype(F32)
+            mask = mask_other[...].reshape(cells, ch)
+            value = jax.nn.sigmoid(both[:, :hid]) * both[:, hid:] * mask
+            buf[kind, s] = value.astype(BF16).reshape(t, t, hid)
 
     def gate_of(u, normed):
         return jax.nn.sigmoid(dot(normed, gate_proj_ref[u]))
@@ -227,10 +244,10 @@
         lax.fori_loop(0, n, body, 0)
         return acc_ref[...].reshape(cells, hid)
 
-    def partials(kind, out_kind, left_major):
+    def partials(kind, out_kind, left_major, fetch):
         def body(d, carry):
             s = after(here(kind), n - d)
-            arrive(kind, s)
+            fetch(kind, s)
             lhs_ref[...] = buf[kind, s].astype(F32)
             acc_ref[...] = jnp.zeros_like(acc_ref)
             multiply(left_major, lambda k: local[k])
@@ -291,11 +308,11 @@
     x0 = pair_ref[...].astype(F32).reshape(cells, ch)
     hat0, inv0, normed0 = enter(0, x0)
     wait_weight(0)
-    share(B0, gated(0, normed0, 2))
+    buf[B0, r] = gated(0, normed0, 2)
     left0 = gated(0, normed0, 0).astype(F32)
     local[...] = turn(left0)
+    partials(B0, H0, True, project_other)
     gate0 = gate_of(0, normed0)
-    partials(B0, H0, True)
     hidden0 = turn(total(H0)).reshape(cells, hid).astype(BF16).astype(F32)
     hid0, hid_inv0, update0, middle = finish(0, hidden0, x0, gate0)
     x1 = middle.astype(BF16).astype(F32)
@@ -305,8 +322,8 @@
     share(A1, gated(1, normed1, 0))
     right1 = gated(1, normed1, 2).astype(F32)
     local[...] = right1
+    partials(A1, H1, False, arrive)
     gate1 = gate_of(1, normed1)
-    partials(A1, H1, False)
     local[...] = turn(right1)
     hidden1 = total(H1).reshape(cells, hid).astype(BF16).astype(F32)
     hid1, hid_inv1, update1, final = finish(1, hidden1, x1, gate1)
@@ -314,20 +331,20 @@
     grad2 = cot_ref[...].astype(F32).reshape(cells, ch)
     d_hidden, d_logit = leave(1, grad2, gate1, update1, hid1, hid_inv1)
     share(D1, d_hidden.astype(BF16).reshape(t, t, hid))
+    partials(D1, L1, True, arrive)
     new_ref[...] = final.astype(BF16).reshape(t, t, ch)
     new_out = pltpu.make_async_copy(new_ref, new_hbm, out_sem.at[0])
     new_out.start()
     d_normed = dot_t(d_logit.astype(BF16), gate_proj_ref[1])
-    partials(D1, L1, True)
     d_right = product(A1, D1)
+    local[...] = left0
     d_left = turn(total(L1)).reshape(cells, hid)
     grad1 = entry(1, grad2, d_left, d_right, d_normed, hat1, inv1)
 
     d_hidden, d_logit = leave(0, grad1, gate0, update0, hid0, hid_inv0)
     share(D0, d_hidden.astype(BF16).reshape(t, t, hid))
-    local[...] = left0
+    partials(D0, R0, False, arrive)
     d_normed = dot_t(d_logit.astype(BF16), gate_proj_ref[0])
-    partials(D0, R0, False)
     d_left = product(D0, B0)
     d_right = total(R0).reshape(cells, hid)
     grad0 = entry(0, grad1, d_left, d_right, d_normed, hat0, inv0)
@@ -338,7 +355,7 @@
     for copy in weight_copies:
         copy.wait_send()
     new_out.wait()
-    for kind in range(KINDS):
+    for kind in range(A1, KINDS):
         for d in range(1, n):
             move(kind, after(here(kind), d), buf.at[kind, here(kind)]).wait_send()
     grad_out.wait()
@@ -383,8 +400,9 @@
             pltpu.SemaphoreType.DMA((8,)),
             pltpu.SemaphoreType.DMA((2,)),
             pltpu.VMEM((KINDS, n, t, t, hid), BF16),
-            pltpu.VMEM((KINDS - H0, n, t, t, hid), BF16),
+            pltpu.VMEM((R0 + 1 - H0, n, t, t, hid), BF16),
             pltpu.VMEM((2, 4, hid, ch), BF16),
+            pltpu.VMEM((t, t, ch), F32),
             pltpu.VMEM((t, t, ch), F32),
             pltpu.VMEM((t, t, hid), F32),
             pltpu.VMEM((t, t, hid), F32),

time: 52.7 us -> 49.7 us (0.943)
  Pallas kernels: 49.1 us -> 46.1 us
    pallas_call x1, Pallas kernels: 49.1 us -> 46.1 us  [shards(): pl.pallas_call(functools.partial(kernel, n, n_chan), out_shape=(jax.Shape...]
where the time goes in v4:
time: 49.7 us; the launch traced here: 49.6 us
  Pallas kernels  46.1 us (93%)
  local copies, waits for them, and re-layouts  2.17 us (4%)
  between operations  1.29 us (3%)
    pallas_call x1, Pallas kernels, shards(): pl.pallas_call(functools.partial(kernel, n, n_chan), out_shape=(jax.Shape...  46.1 us
    unnamed x4, local copies, waits for them, and re-layouts  2.17 us

profile of v4, /device:TPU:3, one launch (start us, length us, event | category | flops | bytes accessed | tf_op | source)
XLA Modules:
  0.0 49.6 jit_solution(10060856957270846629)
XLA Ops:
  1.3 46.1 %shard_map.104 = (bf16[16,16,128]{2,1,0:T(8,128)(2,1)}, f32[16,16,128]{2,1,0:T(8,128)}) custom-call(bf16[16,32,128]{2,1,0:T(8,128)(2,1)} %pair_hbm.1, s32[1]{0:T(128)S(6)} %copy.13.start_ref, s32[1024]{0:T(1024)} %residue_hbm.1, f32[2,128]{1,0:T(2,128)} %in_gain_hbm.1, bf16[2,4,64,128]{3,2,1,0:T(8,128)(2,1)} %bitcast.1, bf16[2,128,128]{2,1,0:T(8,128)(2,1)} %gate_proj_hbm.1, ...), custom_call_target="tpu_custom_call" | custom-call | tf_op jit(solution)/shard_map/pallas_call | solution.py:382
  47.4 0.0 copy-start
  47.4 1.5 %copy.14 = bf16[16,16,128]{2,1,0:T(8,128)(2,1)} copy(bf16[16,16,128]{2,1,0:T(8,128)(2,1)} %get-tuple-element.4) | data formatting | bytes 131072
  48.9 0.0 copy-done
  48.9 0.7 %copy.15 = f32[16,16,128]{2,1,0:T(8,128)} copy(f32[16,16,128]{2,1,0:T(8,128)S(1)} %copy-done) | data formatting | bytes 262144
Async XLA Ops:
  47.4 1.5 %copy-start = (f32[16,16,128]{2,1,0:T(8,128)S(1)}, f32[16,16,128]{2,1,0:T(8,128)}, u32[]{:S(2)}) copy-start(f32[16,16,128]{2,1,0:T(8,128)} %get-tuple-element.5) | copy-start | bytes 393220

commit v5 on v4

--- a/solution.py
+++ b/solution.py
@@ -153,6 +153,10 @@
         )
         pl.when(slot != here(kind))(copy.wait_recv)
 
+    loads[0].wait()
+    for d in range(1, n):
+        move(PAIR, after(r, d), pair_ref).start()
+
     loads[1].wait()
     weight_copies = []
     for u in range(2):
@@ -167,9 +171,6 @@
             )
             copy.start()
             weight_copies.append(copy)
-    loads[0].wait()
-    for d in range(1, n):
-        move(PAIR, after(r, d), pair_ref).start()
     for load in loads[2:]:
         load.wait()
 

time: 49.7 us -> 49.7 us (level)
  no operation moved by 1% of the time
where the time goes in v5:
time: 49.7 us; the launch traced here: 49.6 us
  Pallas kernels  46.1 us (93%)
  local copies, waits for them, and re-layouts  2.17 us (4%)
  between operations  1.29 us (3%)
    pallas_call x1, Pallas kernels, shards(): pl.pallas_call(functools.partial(kernel, n, n_chan), out_shape=(jax.Shape...  46.1 us
    unnamed x4, local copies, waits for them, and re-layouts  2.17 us

profile of v5, /device:TPU:3, one launch (start us, length us, event | category | flops | bytes accessed | tf_op | source)
XLA Modules:
  0.0 49.6 jit_solution(8320594638777487519)
XLA Ops:
  1.3 46.1 %shard_map.104 = (bf16[16,16,128]{2,1,0:T(8,128)(2,1)}, f32[16,16,128]{2,1,0:T(8,128)}) custom-call(bf16[16,32,128]{2,1,0:T(8,128)(2,1)} %pair_hbm.1, s32[1]{0:T(128)S(6)} %copy.13.start_ref, s32[1024]{0:T(1024)} %residue_hbm.1, f32[2,128]{1,0:T(2,128)} %in_gain_hbm.1, bf16[2,4,64,128]{3,2,1,0:T(8,128)(2,1)} %bitcast.1, bf16[2,128,128]{2,1,0:T(8,128)(2,1)} %gate_proj_hbm.1, ...), custom_call_target="tpu_custom_call" | custom-call | tf_op jit(solution)/shard_map/pallas_call | solution.py:383
  47.4 0.0 copy-start
  47.4 1.5 %copy.14 = bf16[16,16,128]{2,1,0:T(8,128)(2,1)} copy(bf16[16,16,128]{2,1,0:T(8,128)(2,1)} %get-tuple-element.4) | data formatting | bytes 131072
  48.9 0.0 copy-done
  48.9 0.7 %copy.15 = f32[16,16,128]{2,1,0:T(8,128)} copy(f32[16,16,128]{2,1,0:T(8,128)S(1)} %copy-done) | data formatting | bytes 262144
Async XLA Ops:
  47.4 1.5 %copy-start = (f32[16,16,128]{2,1,0:T(8,128)S(1)}, f32[16,16,128]{2,1,0:T(8,128)}, u32[]{:S(2)}) copy-start(f32[16,16,128]{2,1,0:T(8,128)} %get-tuple-element.5) | copy-start | bytes 393220
